TPU v7x, 32 devices: a whole 2x2x4 slice. The times are simulated.
32 devices in a mesh: ex: 16 (over z, y, core), grp: 2 (over x).
Axes of the slice: x: 2, y: 2, z: 4, core: 2. Of those that a mesh axis runs over, the one named last changes fastest.
Arguments:
- queries: bfloat16 [4096, 65536], P('ex', 'grp'), may hold values from -6 to 6
- inv_in: bfloat16 [16, 64, 64], P('grp'), as said below
- inv_out: bfloat16 [16, 64, 64], P('grp'), as said below
- store: bfloat16 [8192, 65536], P('ex', 'grp'), may hold values from -0.0234375 to 0.0234375
- listed: int32 [128, 24], P('ex'), may hold values from 0 to 1, as said below
Outputs:
- scores: float32 [3, 4096, 512], P(None, ('ex', 'grp'))
Inputs may be any that keep to these rules, and one draw needn't show every extreme that they name: Entries are 0 or 1; every query block lists column 0 and column 23, the other numbers listed differ from block to block and from ex block to ex block, and some query block lists all 24. `inv_in`: each matrix is symmetric and positive definite. `inv_out`: each matrix is symmetric and positive definite.
All inputs are finite; a program needn't handle non-finite values.
Results may differ from a plain program's by a relative error of at most 0.0041.
Values may be sent and summed in bfloat16 or wider, within the bound.
No kernel may reach another device: no remote copies, remote signals or barrier semaphores. Data moves between devices by JAX's collectives and lax.ppermute only.
A program may use at most 192 MiB of HBM per device.

v0:
```python
import jax
import jax.numpy as jnp
from jax import lax
from jax.sharding import PartitionSpec as P

QB = 32
SUB = 64


def shifted(value, axis, steps):
    count = lax.axis_size(axis)
    pairs = [(source, (source + steps) % count) for source in range(count)]
    return lax.ppermute(value, axis, pairs)


def precondition(queries, inv_in, inv_out):
    count = queries.shape[0]
    modules = inv_in.shape[0]
    side = inv_in.shape[1]
    query_part = queries.reshape(count, modules, side, side)
    left = jnp.einsum(
        "mab,qmbc->qmac", inv_in, query_part, preferred_element_type=jnp.float32
    ).astype(jnp.bfloat16)
    ready = jnp.einsum("qmac,mcd->qmad", left, inv_out, preferred_element_type=jnp.float32)
    return ready.reshape(count, modules * side * side).astype(jnp.bfloat16)


def widen(listed_rows, first, count):
    piece = lax.slice_in_dim(listed_rows, first, first + count, axis=1).astype(jnp.float32)
    blocks = piece.shape[0]
    full = jnp.broadcast_to(piece[:, None, :, None], (blocks, QB, count, SUB))
    return full.reshape(blocks * QB, count * SUB)


def score(ready, slab, listed_rows, window):
    blocks = slab.shape[0] // SUB
    part = lax.dot_general(
        ready, slab, (((1,), (1,)), ((), ())), preferred_element_type=jnp.float32
    )
    return part * widen(listed_rows, window * blocks, blocks)


def body(queries, inv_in, inv_out, store, listed):
    ready = precondition(queries, inv_in, inv_out)
    own_part = score(ready, store, listed, 1)
    lower_items = shifted((ready, listed), "ex", 1)
    upper_items = shifted((ready, listed), "ex", -1)
    visit_upper = score(upper_items[0], store, upper_items[1], 0)
    visit_lower = score(lower_items[0], store, lower_items[1], 2)
    stacked = jnp.stack([visit_upper, own_part, visit_lower])
    summed = lax.psum_scatter(stacked, "grp", scatter_dimension=1, tiled=True)
    upper_sum = shifted(summed[0], "ex", 1)
    lower_sum = shifted(summed[2], "ex", -1)
    summed = jnp.stack([upper_sum, summed[1], lower_sum])
    return summed


def solution(mesh):
    in_specs = (
        P("ex", "grp"),
        P("grp", None, None),
        P("grp", None, None),
        P("ex", "grp"),
        P("ex", None),
    )
    out_specs = P(None, ("ex", "grp"), None)
    return jax.shard_map(body, mesh=mesh, in_specs=in_specs, out_specs=out_specs, check_vma=False)
```

profile of v0, /device:TPU:1, one launch (start us, length us, event | category | flops | bytes accessed | tf_op | source)
XLA Modules:
  0.0 523.0 jit_solution(17039038715877887827)
XLA Ops:
  6.5 0.0 copy-start
  6.5 0.0 reduce-scatter.2.cloned.1.call-start
  6.5 22.3 %copy.7 = bf16[256,32768]{0,1:T(8,128)(2,1)} copy(bf16[256,32768]{1,0:T(8,128)(2,1)} %param.5) | data formatting | bytes 33554432 | tf_op args[0]
  28.9 0.0 copy-done
  28.9 0.0 copy-start.2
  28.9 22.9 %fusion.3 = bf16[8,256,64,64]{1,3,2,0:T(8,128)(2,1)} fusion(bf16[256,8,64,64]{0,3,2,1:T(8,128)(2,1)} %bitcast.43, bf16[8,64,64]{2,1,0:T(8,128)(2,1)S(1)} %copy-done), kind=kOutput, calls=%fused_computation.3 | convolution fusion | flops 1073741824 | bytes 33619968 | tf_op jit(solution)/shard_map/mab,qmbc->qmac/dot_general | solution.py:21
  51.7 0.0 copy-done.2
  51.7 0.0 copy-start.3
  51.7 20.8 %fusion.5 = bf16[8,256,64,64]{1,3,2,0:T(8,128)(2,1)} fusion(bf16[8,256,64,64]{1,3,2,0:T(8,128)(2,1)} %fusion.3, bf16[8,64,64]{2,1,0:T(8,128)(2,1)S(1)} %copy-done.2), kind=kOutput, calls=%fused_computation.5 | convolution fusion | flops 1082130432 | bytes 33619968 | tf_op jit(solution)/shard_map/qmac,mcd->qmad/dot_general | solution.py:24
  72.5 2.6 collective-permute-start.2
  75.1 0.0 collective-permute-start
  75.1 0.0 copy-done.3
  75.1 2.9 collective-permute-start.1
  78.0 0.0 collective-permute-start.3
  78.0 0.1 slice_convert_fusion.1
  78.1 0.1 broadcast_in_dim.7
  78.2 0.3 reshape.19
  78.5 18.8 %fusion.9 = f32[1,256,512]{2,1,0:T(8,128)S(1)} fusion(f32[256,512]{1,0:T(8,128)S(1)} %reshape.19, bf16[256,32768]{0,1:T(8,128)(2,1)} %bitcast.6, bf16[512,32768]{1,0:T(8,128)(2,1)} %param.8), kind=kOutput, calls=%fused_computation.10 | convolution fusion | flops 8590065664 | bytes 51380224 | tf_op jit(solution)/shard_map/dot_general | solution.py:37
  97.3 338.2 %collective-permute-done.3 = s32[8,24]{1,0:T(8,128)S(1)} collective-permute-done((s32[8,24]{1,0:T(8,128)S(1)}, s32[8,24]{1,0:T(8,128)S(1)}, u32[]{:S(2)}, u32[]{:S(2)}) %collective-permute-start.3) | collective-permute-done | bytes 800 | tf_op jit(solution)/shard_map/ppermute | solution.py:13
  435.5 0.1 slice_convert_fusion
  435.6 0.1 broadcast_in_dim.8
  435.7 0.3 reshape.20
  436.0 2.0 collective-permute-done.1
  438.0 0.1 broadcast_in_dim.6
  438.2 0.3 reshape.18
  438.4 0.0 collective-permute-done.2
  438.4 18.8 %fusion.8 = f32[1,256,512]{2,1,0:T(8,128)S(1)} fusion(f32[256,512]{1,0:T(8,128)S(1)} %reshape.20, bf16[256,32768]{0,1:T(8,128)(2,1)} %collective-permute-done.2, bf16[512,32768]{1,0:T(8,128)(2,1)} %param.8), kind=kOutput, calls=%fused_computation.8 | convolution fusion | flops 8590065664 | bytes 51380224 | tf_op jit(solution)/shard_map/dot_general | solution.py:37
  457.3 0.0 collective-permute-done
  457.3 0.0 copy-start.1
  457.3 18.9 %fusion.10 = f32[1,256,512]{2,1,0:T(8,128)S(1)} fusion(f32[256,512]{1,0:T(8,128)S(1)} %reshape.18, bf16[256,32768]{0,1:T(8,128)(2,1)} %collective-permute-done, bf16[512,32768]{1,0:T(8,128)(2,1)} %param.8), kind=kOutput, calls=%fused_computation.12 | convolution fusion | flops 8590065664 | bytes 51380224 | tf_op jit(solution)/shard_map/dot_general | solution.py:37
  476.2 1.3 pad_maximum_fusion
  477.5 0.0 reduce-scatter.2.cloned.1.call-update
  477.5 26.2 %reduce-scatter.2.cloned.1.call-done = f32[3,128,512]{2,1,0:T(8,128)} async-done(((f32[3,256,512]{2,1,0:T(8,128)}), f32[3,128,512]{2,1,0:T(8,128)}) %reduce-scatter.2.cloned.1.call-update) | async-done | bytes 786448 | tf_op jit(solution)/shard_map/reduce_scatter | solution.py:51
  503.7 1.2 slice_bitcast_fusion.1
  504.8 1.8 collective-permute-start.4
  506.6 0.0 collective-permute-start.5
  506.6 3.3 collective-permute-done.4
  509.9 5.3 %collective-permute-done.5 = f32[128,512]{1,0:T(8,128)S(1)} collective-permute-done((f32[128,512]{1,0:T(8,128)S(1)}, f32[128,512]{1,0:T(8,128)S(1)}, u32[]{:S(2)}, u32[]{:S(2)}) %collective-permute-start.5) | collective-permute-done | bytes 262176 | tf_op jit(solution)/shard_map/ppermute | solution.py:13
  515.2 0.9 pad_maximum_fusion.1
  516.2 0.0 copy-done.1
  (1 shorter events, 0.0 us)
Async XLA Ops:
  6.5 22.3 %copy-start = (bf16[8,64,64]{2,1,0:T(8,128)(2,1)S(1)}, bf16[8,64,64]{2,1,0:T(8,128)(2,1)}, u32[]{:S(2)}) copy-start(bf16[8,64,64]{2,1,0:T(8,128)(2,1)} %param.6) | copy-start | bytes 196612
  6.5 497.1 %reduce-scatter.2.cloned.1.call-start = ((), (), s32[]{:S(2)}) async-start(), calls=%async_computation.1 | async-start | bytes 2359296 | tf_op jit(solution)/shard_map/reduce_scatter | solution.py:51
  28.9 22.9 %copy-start.2 = (bf16[8,64,64]{2,1,0:T(8,128)(2,1)S(1)}, bf16[8,64,64]{2,1,0:T(8,128)(2,1)}, u32[]{:S(2)}) copy-start(bf16[8,64,64]{2,1,0:T(8,128)(2,1)} %param.7) | copy-start | bytes 196612
  51.7 23.4 %copy-start.3 = (s32[8,24]{1,0:T(8,128)S(1)}, s32[8,24]{1,0:T(8,128)}, u32[]{:S(2)}) copy-start(s32[8,24]{1,0:T(8,128)} %param.9) | copy-start | bytes 2308
  72.5 365.9 %collective-permute-start.2 = (bf16[256,32768]{0,1:T(8,128)(2,1)}, bf16[256,32768]{0,1:T(8,128)(2,1)}, u32[]{:S(2)}, u32[]{:S(2)}) collective-permute-start(bf16[256,32768]{0,1:T(8,128)(2,1)} %bitcast.6), channel_id=1, source_target_pairs={{0,2},{2,4},{4,6},{6,8},{8,10},{10,12},{12,14},{14,16},{16,18},{18... | collective-permute-start | bytes 50331656 | tf_op jit(solution)/shard_map/ppermute | solution.py:13
  75.1 382.2 %collective-permute-start = (bf16[256,32768]{0,1:T(8,128)(2,1)}, bf16[256,32768]{0,1:T(8,128)(2,1)}, u32[]{:S(2)}, u32[]{:S(2)}) collective-permute-start(bf16[256,32768]{0,1:T(8,128)(2,1)} %bitcast.6), channel_id=1, source_target_pairs={{0,30},{2,0},{4,2},{6,4},{8,6},{10,8},{12,10},{14,12},{16,14},{18,... | collective-permute-start | bytes 50331656 | tf_op jit(solution)/shard_map/ppermute | solution.py:13
  75.1 362.9 %collective-permute-start.1 = (s32[8,24]{1,0:T(8,128)S(1)}, s32[8,24]{1,0:T(8,128)S(1)}, u32[]{:S(2)}, u32[]{:S(2)}) collective-permute-start(s32[8,24]{1,0:T(8,128)S(1)} %copy-done.3), channel_id=1, source_target_pairs={{0,30},{2,0},{4,2},{6,4},{8,6},{10,8},{12,10},{14,12},{16,14},{18,... | collective-permute-start | bytes 2312 | tf_op jit(solution)/shard_map/ppermute | solution.py:13
  78.0 357.5 %collective-permute-start.3 = (s32[8,24]{1,0:T(8,128)S(1)}, s32[8,24]{1,0:T(8,128)S(1)}, u32[]{:S(2)}, u32[]{:S(2)}) collective-permute-start(s32[8,24]{1,0:T(8,128)S(1)} %copy-done.3), channel_id=1, source_target_pairs={{0,2},{2,4},{4,6},{6,8},{8,10},{10,12},{12,14},{14,16},{16,18},{18... | collective-permute-start | bytes 2312 | tf_op jit(solution)/shard_map/ppermute | solution.py:13
  457.3 58.9 %copy-start.1 = (bf16[8,64,64]{2,1,0:T(8,128)(2,1)S(1)}, bf16[8,64,64]{2,1,0:T(8,128)(2,1)}, u32[]{:S(2)}) copy-start(bf16[8,64,64]{2,1,0:T(8,128)(2,1)} %param.6) | copy-start | bytes 196612
  504.8 5.1 collective-permute-start.4
  506.6 8.6 %collective-permute-start.5 = (f32[128,512]{1,0:T(8,128)S(1)}, f32[128,512]{1,0:T(8,128)S(1)}, u32[]{:S(2)}, u32[]{:S(2)}) collective-permute-start(f32[128,512]{1,0:T(8,128)S(1)} %get-tuple-element.6), channel_id=1, source_target_pairs={{0,30},{2,0},{4,2},{6,4},{8,6},{10,8},{12,10},{14,12},{16,14},{18,... | collective-permute-start | bytes 786440 | tf_op jit(solution)/shard_map/ppermute | solution.py:13
Sparse Core Ops, SparseCore 0:
  477.6 26.0 reduce-scatter.1
where the time goes:
time: 524 us; the launch traced here: 523 us
  waiting for transfers between devices  375 us (72%)
  matrix products  100 us (19%)
  local copies, waits for them, and re-layouts  24.7 us (5%)
  between operations  13.5 us (3%)
  starting transfers between devices  7.31 us (1%)
    ppermute x6, waiting for transfers between devices, shifted(): return lax.ppermute(value, axis, pairs)  349 us
    dot_general x3, matrix products, score(): lax.dot_general(ready, slab, (((1,), (1,)), ((), ())), preferred_element_...  56.5 us
    reduce_scatter x1, waiting for transfers between devices, body(): summed = lax.psum_scatter(stacked, 'grp', scatter_dimension=1, tiled=True)  26.2 us
    dot_general x1, matrix products, precondition(): jnp.einsum('mab,qmbc->qmac', inv_in, query_part, preferred_element_type=j...  22.9 us
    unnamed x9, local copies, waits for them, and re-layouts  22.3 us
    dot_general x1, matrix products, precondition(): jnp.einsum('qmac,mcd->qmad', left, inv_out, preferred_element_type=jnp.fl...  20.8 us
  transfers between devices with their start and end apart: 7, of which 5 were waited for; matrix products, arithmetic and copies ran while one was open for 7% of the time, Pallas kernels for 0%

commit v1 on v0

v1 whole, which is shorter than its diff:
```python
import functools

import jax
import jax.numpy as jnp
from jax import lax
from jax.experimental import pallas as pl
from jax.experimental.pallas import tpu as pltpu
from jax.sharding import PartitionSpec as P

QB = 32
SUB = 64
CHUNKS = (1, 3, 6, 2, 4)
PIECES = (3, 3, 2)
WIDE = 256
LOW = 8
VMEM = 56 * 1024 * 1024
NT = (((1,), (1,)), ((), ()))
TN = (((0,), (0,)), ((), ()))


def spread(matrix, rows_of, columns_of, keep):
    tall = jnp.dot(rows_of, matrix, preferred_element_type=jnp.float32)
    full = lax.dot_general(
        tall.astype(jnp.bfloat16), columns_of, NT, preferred_element_type=jnp.float32
    )
    return jnp.where(keep, full, 0.0).astype(jnp.bfloat16)


def precondition(x, inv_in, inv_out, turned, left):
    n, size = x.shape
    side = inv_in.shape[0]
    high = side // LOW
    per = WIDE // side

    def iota(shape, dim):
        return lax.broadcasted_iota(jnp.int32, shape, dim)

    def unit(rows, columns, test):
        hit = test(iota((rows, columns), 0), iota((rows, columns), 1))
        return jnp.where(hit, 1.0, 0.0).astype(jnp.bfloat16)

    identity = unit(WIDE, WIDE, lambda r, c: r == c)
    for block in range(size // WIDE):
        part = lax.dot_general(
            identity,
            x[:, block * WIDE : (block + 1) * WIDE],
            NT,
            preferred_element_type=jnp.float32,
        )
        turned[block * per : (block + 1) * per] = part.reshape(per, high, LOW, n)

    span = side * LOW
    expand = unit(span, side, lambda r, c: r // LOW == c)
    square = (span, span)
    factor = spread(inv_in, expand, expand, iota(square, 0) % LOW == iota(square, 1) % LOW)
    for part in range(high):
        piece = turned[:, part].reshape(span, n).astype(jnp.bfloat16)
        result = jnp.dot(factor, piece, preferred_element_type=jnp.float32)
        left[:, part] = result.astype(jnp.bfloat16).astype(jnp.float32).reshape(side, LOW, n)

    repeat = unit(WIDE, side, lambda r, c: r % side == c)
    square = (WIDE, WIDE)
    factor = spread(inv_out, repeat, repeat, iota(square, 0) // side == iota(square, 1) // side)
    blocks = []
    for block in range(size // WIDE):
        piece = left[block * per : (block + 1) * per].reshape(WIDE, n).astype(jnp.bfloat16)
        result = lax.dot_general(piece, factor, TN, preferred_element_type=jnp.float32)
        blocks.append(result.astype(jnp.bfloat16))
    return blocks


def add_scores(rows, slab, out_ref):
    part = lax.dot_general(rows, slab, NT, preferred_element_type=jnp.float32)

    @pl.when(pl.program_id(0) == 0)
    def _():
        out_ref[...] = part.reshape(out_ref.shape)

    @pl.when(pl.program_id(0) != 0)
    def _():
        out_ref[...] += part.reshape(out_ref.shape)


def own_kernel(bounds, x_ref, in_ref, out_ref, slab_ref, *rest):
    chunks, scores_ref, (turned, left, held) = rest[:-4], rest[-4], rest[-3:]
    n = x_ref.shape[0]
    groups = scores_ref.shape[0]
    rows = n // groups
    blocks = precondition(x_ref[...], in_ref[0], out_ref[0], turned, left)
    for index, block in enumerate(blocks):
        cut = pl.ds(index * WIDE, WIDE)
        held[:, cut] = block
        for chunk, low, top in zip(chunks, bounds[:-1], bounds[1:]):
            for group in range(groups):
                chunk[group, :, cut] = block[group * rows + low : group * rows + top]
    add_scores(held[...], slab_ref[...], scores_ref)


def own(queries, inv_in, inv_out, store, groups, bounds):
    n, dims = queries.shape
    modules, side, _ = inv_in.shape
    size = side * side
    examples = store.shape[0]
    small = pl.BlockSpec((1, side, side), lambda m: (m, 0, 0))
    sizes = [top - low for low, top in zip(bounds[:-1], bounds[1:])]
    *chunks, mine = pl.pallas_call(
        functools.partial(own_kernel, bounds),
        grid=(modules,),
        in_specs=[
            pl.BlockSpec((n, size), lambda m: (0, m)),
            small,
            small,
            pl.BlockSpec((examples, size), lambda m: (0, m)),
        ],
        out_specs=[pl.BlockSpec((groups, c, size), lambda m: (0, 0, m)) for c in sizes]
        + [pl.BlockSpec((groups, n // groups, examples), lambda m: (0, 0, 0))],
        out_shape=[jax.ShapeDtypeStruct((groups, c, dims), jnp.bfloat16) for c in sizes]
        + [jax.ShapeDtypeStruct((groups, n // groups, examples), jnp.float32)],
        scratch_shapes=[
            pltpu.VMEM((side, side // LOW, LOW, n), jnp.float32),
            pltpu.VMEM((side, side // LOW, LOW, n), jnp.float32),
            pltpu.VMEM((n, size), jnp.bfloat16),
        ],
        compiler_params=pltpu.CompilerParams(vmem_limit_bytes=VMEM),
        name="own",
    )(queries, inv_in, inv_out, store)
    return chunks, mine


def visit_raw_kernel(count, *refs):
    pieces = refs[:count]
    in_ref, out_ref, slab_ref, scores_ref, turned, left, held = refs[count:]
    _, groups, rows, _ = scores_ref.shape
    at = 0
    for piece in pieces:
        n = piece.shape[0] * piece.shape[1]
        held[at : at + n] = piece[...].reshape(n, piece.shape[2])
        at += n
    blocks = precondition(held[...], in_ref[0], out_ref[0], turned, left)
    for index, block in enumerate(blocks):
        held[:, index * WIDE : (index + 1) * WIDE] = block
    add_scores(held[...], slab_ref[...], scores_ref)


def visit_raw(raw, inv_in, inv_out, store):
    modules, side, _ = inv_in.shape
    size = side * side
    examples = store.shape[0]
    pieces = [upper for upper, _ in raw] + [lower for _, lower in raw]
    groups = pieces[0].shape[0]
    counts = [upper.shape[1] for upper, _ in raw]
    n = 2 * groups * sum(counts)
    small = pl.BlockSpec((1, side, side), lambda m: (m, 0, 0))
    scores = pl.pallas_call(
        functools.partial(visit_raw_kernel, len(pieces)),
        grid=(modules,),
        in_specs=[pl.BlockSpec((*p.shape[:2], size), lambda m: (0, 0, m)) for p in pieces]
        + [small, small, pl.BlockSpec((examples, size), lambda m: (0, m))],
        out_specs=pl.BlockSpec((2, groups, sum(counts), examples), lambda m: (0, 0, 0, 0)),
        out_shape=jax.ShapeDtypeStruct((2, groups, sum(counts), examples), jnp.float32),
        scratch_shapes=[
            pltpu.VMEM((side, side // LOW, LOW, n), jnp.float32),
            pltpu.VMEM((side, side // LOW, LOW, n), jnp.float32),
            pltpu.VMEM((n, size), jnp.bfloat16),
        ],
        compiler_params=pltpu.CompilerParams(vmem_limit_bytes=VMEM),
        name="visit_raw",
    )(*pieces, inv_in, inv_out, store)
    flat = scores.reshape(2, -1, examples)
    at, found = 0, []
    for count in counts:
        found.append(flat[:, at : at + groups * count].reshape(2, groups, count, examples))
        at += groups * count
    return jnp.concatenate(found, axis=2)


def visit_kernel(upper_ref, lower_ref, slab_ref, scores_ref):
    groups, rows, width = upper_ref.shape
    both = jnp.concatenate(
        [upper_ref[...].reshape(groups * rows, width), lower_ref[...].reshape(groups * rows, width)]
    )
    add_scores(both, slab_ref[...], scores_ref)


def visit(upper, lower, store, first, unit):
    groups, rows, width = upper.shape
    examples = store.shape[0]
    block = pl.BlockSpec((groups, rows, unit), lambda s: (0, 0, s))
    return pl.pallas_call(
        visit_kernel,
        grid=(width // unit,),
        in_specs=[block, block, pl.BlockSpec((examples, unit), lambda s: (0, s + first))],
        out_specs=pl.BlockSpec((2, groups, rows, examples), lambda s: (0, 0, 0, 0)),
        out_shape=jax.ShapeDtypeStruct((2, groups, rows, examples), jnp.float32),
        compiler_params=pltpu.CompilerParams(vmem_limit_bytes=VMEM),
        name="visit",
    )(upper, lower, store)


def shifted(value, axis, steps):
    count = lax.axis_size(axis)
    pairs = [(source, (source + steps) % count) for source in range(count)]
    return lax.ppermute(value, axis, pairs)


def grp_sum(part, dim):
    groups = lax.axis_size("grp")
    me = lax.axis_index("grp")
    total = lax.dynamic_index_in_dim(part, me, dim, keepdims=False)
    for turn in range(1, groups):
        share = lax.dynamic_index_in_dim(part, (me + turn) % groups, dim, keepdims=False)
        total = total + shifted(share, "grp", turn)
    return total


def to_owner(part, steps):
    ex = lax.axis_size("ex")
    groups = lax.axis_size("grp")
    me = lax.axis_index("grp")
    total = None
    for turn in range(groups):
        share = lax.dynamic_index_in_dim(part, (me + turn) % groups, 0, keepdims=False)
        pairs = [
            (b * groups + g, ((b + steps) % ex) * groups + (g + turn) % groups)
            for b in range(ex)
            for g in range(groups)
        ]
        arrived = lax.ppermute(share, ("ex", "grp"), pairs)
        total = arrived if total is None else total + arrived
    return total


def body(queries, inv_in, inv_out, store, listed):
    groups = lax.axis_size("grp")
    rows = queries.shape[0] // groups
    dims = queries.shape[1]
    unit = dims // sum(PIECES)
    bounds = [0]
    for part in CHUNKS:
        bounds.append(bounds[-1] + rows * part // sum(CHUNKS))
    together = lax.optimization_barrier

    def send(value):
        return shifted(value, "ex", -1), shifted(value, "ex", 1)

    split = queries.reshape(groups, rows, dims)
    first = lax.optimization_barrier(split[:, : bounds[1]])
    raw_one = send(first)
    raw_two = send(split[:, bounds[1] : bounds[2]])
    queries, raw_one = together((queries, raw_one))
    (a, b, c), mine = own(queries, inv_in, inv_out, store, groups, bounds[2:])
    cuts = []
    start = 0
    for count in PIECES:
        cuts.append(c[..., start * unit : (start + count) * unit])
        start += count

    came_a = send(a)
    b, raw_two = together((b, raw_two))
    came_b = send(b)
    scores_raw = visit_raw([raw_one, raw_two], inv_in, inv_out, store)
    cut, came_a, scores_raw = together((cuts[0], came_a, scores_raw))
    came_c = [send(cut)]
    scores_a = visit(*came_a, store, 0, unit)
    cut, came_b, scores_a = together((cuts[1], came_b, scores_a))
    came_c.append(send(cut))
    scores_b = visit(*came_b, store, 0, unit)
    cut, came_c[0], scores_b = together((cuts[2], came_c[0], scores_b))
    came_c.append(send(cut))
    both = grp_sum(jnp.concatenate([scores_raw, scores_a, scores_b], axis=2), 1)
    part = visit(*came_c[0], store, 0, unit)
    both, came_c[1] = together((both, came_c[1]))
    upper_scores = [shifted(both[0], "ex", 1)]
    lower_scores = [shifted(both[1], "ex", -1)]
    part = part + visit(*came_c[1], store, PIECES[0], unit)
    own_scores = grp_sum(mine, 0)
    part = part + visit(*came_c[2], store, PIECES[0] + PIECES[1], unit)
    upper_scores.append(to_owner(part[0], 1))
    lower_scores.append(to_owner(part[1], -1))

    scores = jnp.stack(
        [jnp.concatenate(upper_scores), own_scores, jnp.concatenate(lower_scores)]
    )
    return scores * mask(listed, rows, scores.shape[2])


def mask(listed, rows, examples):
    blocks = examples // SUB
    full = jnp.repeat(listed.astype(jnp.float32), QB, axis=0)
    start = lax.axis_index("grp") * rows
    mine = lax.dynamic_slice_in_dim(full, start, rows, 0)
    mine = mine.reshape(rows, 3, blocks).transpose(1, 0, 2)
    return jnp.repeat(mine, SUB, axis=2)


def solution(mesh):
    in_specs = (
        P("ex", "grp"),
        P("grp", None, None),
        P("grp", None, None),
        P("ex", "grp"),
        P("ex", None),
    )
    out_specs = P(None, ("ex", "grp"), None)
    return jax.shard_map(body, mesh=mesh, in_specs=in_specs, out_specs=out_specs, check_vma=False)
```

time: 524 us -> 458 us (0.87); the launches traced: 523 us -> 451 us
  waiting for transfers between devices: 375 us -> 222 us
  Pallas kernels: 0 us -> 136 us
  matrix products: 100 us -> 0 us
  starting transfers between devices: 7.31 us -> 73.2 us
  between operations: 13.5 us -> 0.29 us
  local copies, waits for them, and re-layouts: 24.7 us -> 17.7 us
    ppermute x6 -> x18, waiting for transfers between devices: 349 us -> 207 us  [shifted(): return lax.ppermute(value, axis, pairs)]
    pallas_call x0 -> x7, Pallas kernels: none -> 136 us  [the longest x5 61.9 us: visit(): pl.pallas_call(visit_kernel, grid=(width // unit,), in_specs=[block, bloc...]
    dot_general x5 -> x0, matrix products: 100 us -> none  [the longest x3 56.5 us: score(): lax.dot_general(ready, slab, (((1,), (1,)), ((), ())), preferred_element_...]
    ppermute x0 -> x4, starting transfers between devices: none -> 34 us  [to_owner(): arrived = lax.ppermute(share, ('ex', 'grp'), pairs)]
    ppermute x6 -> x18, starting transfers between devices: 7.31 us -> 39.2 us  [shifted(): return lax.ppermute(value, axis, pairs)]
    reduce_scatter x1 -> x0, waiting for transfers between devices: 26.2 us -> none  [body(): summed = lax.psum_scatter(stacked, 'grp', scatter_dimension=1, tiled=True)]
    unnamed x9 -> x22, local copies, waits for them, and re-layouts: 22.3 us -> 1.96 us
    ppermute x0 -> x4, waiting for transfers between devices: none -> 15.3 us  [to_owner(): arrived = lax.ppermute(share, ('ex', 'grp'), pairs)]
  transfers between devices with their start and end apart: 7 -> 22, of which waited for: 5 -> 10; matrix products, arithmetic and copies ran while one was open for 7% -> 3% of each run, Pallas kernels for 0% -> 30%
where the time goes in v1:
time: 458 us; the launch traced here: 451 us
  waiting for transfers between devices  222 us (48%)
  Pallas kernels  136 us (30%)
  starting transfers between devices  73.2 us (16%)
  local copies, waits for them, and re-layouts  17.7 us (4%)
    ppermute x18, waiting for transfers between devices, shifted(): return lax.ppermute(value, axis, pairs)  207 us
    pallas_call x5, Pallas kernels, visit(): pl.pallas_call(visit_kernel, grid=(width // unit,), in_specs=[block, bloc...  61.9 us
    ppermute x18, starting transfers between devices, shifted(): return lax.ppermute(value, axis, pairs)  39.2 us
    pallas_call x1, Pallas kernels, own(): pl.pallas_call(functools.partial(own_kernel, bounds), grid=(modules,), in...  37.6 us
    pallas_call x1, Pallas kernels, visit_raw(): pl.pallas_call(functools.partial(visit_raw_kernel, len(pieces)), grid=(mo...  36.3 us
    ppermute x4, starting transfers between devices, to_owner(): arrived = lax.ppermute(share, ('ex', 'grp'), pairs)  34 us
    ppermute x4, waiting for transfers between devices, to_owner(): arrived = lax.ppermute(share, ('ex', 'grp'), pairs)  15.3 us
  transfers between devices with their start and end apart: 22, of which 10 were waited for; matrix products, arithmetic and copies ran while one was open for 3% of the time, Pallas kernels for 30%

profile of v1, /device:TPU:1, one launch (start us, length us, event | category | flops | bytes accessed | tf_op | source)
XLA Modules:
  0.0 451.1 jit_solution(7527346809824643158)
XLA Ops:
  0.0 1.3 slice.44
  1.3 2.7 collective-permute-start.1
  4.0 3.7 slice.45
  7.7 1.7 collective-permute-start.5
  9.5 1.2 collective-permute-start.4
  10.7 50.0 %collective-permute-done.1.refs_2_ = bf16[2,8,32768]{2,1,0:T(8,128)(2,1)S(1)} collective-permute-done((bf16[2,8,32768]{2,1,0:T(8,128)(2,1)S(1)}, bf16[2,8,32768]{2,1,0:T(8,128)(2,1)S(1)}, u32[]{:S(2)}, u32[]{:S(2)}) %collective-permute-start.1) | collective-permute-done | bytes 1048608 | tf_op jit(solution)/shard_map/ppermute | solution.py:203
  60.7 1.0 copy-done.7
  61.7 1.6 collective-permute-done.refs_0_
  63.2 37.6 %own.1 = (bf16[2,48,32768]{2,1,0:T(8,128)(2,1)}, bf16[2,16,32768]{2,1,0:T(8,128)(2,1)}, bf16[2,32,32768]{2,1,0:T(8,128)(2,1)}, f32[2,128,512]{2,1,0:T(8,128)}) custom-call(bf16[256,32768]{1,0:T(8,128)(2,1)} %x_ref, bf16[8,64,64]{2,1,0:T(8,128)(2,1)} %refs_4_.1, bf16[8,64,64]{2,1,0:T(8,128)(2,1)} %refs_5_.1, bf16[512,32768]{1,0:T(8,128)(2,1)} %slab_ref.11), custom_call_target="tpu_custom_call" | custom-call | tf_op jit(solution)/shard_map/own/pallas_call | solution.py:106
  100.8 1.0 collective-permute-start.3
  101.8 62.6 %collective-permute-done.4.refs_1_ = bf16[2,24,32768]{2,1,0:T(8,128)(2,1)} collective-permute-done((bf16[2,24,32768]{2,1,0:T(8,128)(2,1)}, bf16[2,24,32768]{2,1,0:T(8,128)(2,1)}, u32[]{:S(2)}, u32[]{:S(2)}) %collective-permute-start.4) | collective-permute-done | bytes 3145760 | tf_op jit(solution)/shard_map/ppermute | solution.py:203
  164.4 0.5 collective-permute-start.6
  164.9 3.3 fusion.1
  168.2 36.3 %visit_raw.1 = f32[2,2,32,512]{3,2,1,0:T(8,128)} custom-call(bf16[2,8,32768]{2,1,0:T(8,128)(2,1)} %collective-permute-done.refs_0_, bf16[2,24,32768]{2,1,0:T(8,128)(2,1)} %collective-permute-done.4.refs_1_, bf16[2,8,32768]{2,1,0:T(8,128)(2,1)} %copy-done.7, bf16[2,24,32768]{2,1,0:T(8,128)(2,1)} %collective-permute-done.5.refs_3_, ...), custom_call_target="tpu_custom_call" | custom-call | tf_op jit(solution)/shard_map/visit_raw/pallas_call | solution.py:154
  204.5 0.9 slice.47
  205.5 0.8 slice_bitcast_fusion.2
  206.4 64.7 %collective-permute-done.2.upper_ref = bf16[2,48,32768]{2,1,0:T(8,128)(2,1)} collective-permute-done((bf16[2,48,32768]{2,1,0:T(8,128)(2,1)}, bf16[2,48,32768]{2,1,0:T(8,128)(2,1)}, u32[]{:S(2)}, u32[]{:S(2)}) %collective-permute-start.2) | collective-permute-done | bytes 6291488 | tf_op jit(solution)/shard_map/ppermute | solution.py:203
  271.1 0.5 collective-permute-start.8
  271.6 20.0 %visit.5 = f32[2,2,48,512]{3,2,1,0:T(8,128)} custom-call(bf16[2,48,32768]{2,1,0:T(8,128)(2,1)} %collective-permute-done.2.upper_ref, bf16[2,48,32768]{2,1,0:T(8,128)(2,1)} %copy-done, bf16[512,32768]{1,0:T(8,128)(2,1)} %slab_ref.11), custom_call_target="tpu_custom_call" | custom-call | tf_op jit(solution)/shard_map/visit/pallas_call | solution.py:189
  291.6 1.9 collective-permute-done.6.upper_ref
  293.6 0.5 collective-permute-start.11
  294.1 2.2 slice.39
  296.3 17.7 %visit.6 = f32[2,2,16,512]{3,2,1,0:T(8,128)} custom-call(bf16[2,16,32768]{2,1,0:T(8,128)(2,1)} %collective-permute-done.6.upper_ref, bf16[2,16,32768]{2,1,0:T(8,128)(2,1)} %collective-permute-done.7.lower_ref, bf16[512,32768]{1,0:T(8,128)(2,1)} %slab_ref.11), custom_call_target="tpu_custom_call" | custom-call | tf_op jit(solution)/shard_map/visit/pallas_call | solution.py:189
  314.1 24.4 %collective-permute-done.8.upper_ref = bf16[2,32,12288]{2,1,0:T(8,128)(2,1)} collective-permute-done((bf16[2,32,12288]{2,1,0:T(8,128)(2,1)S(1)}, bf16[2,32,12288]{2,1,0:T(8,128)(2,1)}, u32[]{:S(2)}, u32[]{:S(2)}) %collective-permute-start.8) | collective-permute-done | bytes 1572896 | tf_op jit(solution)/shard_map/ppermute | solution.py:203
  338.5 0.5 collective-permute-start.14
  339.0 0.9 constant_dynamic-update-slice_fusion
  340.0 0.9 copy-done.3
  340.8 0.8 dynamic-slice_bitcast_fusion
  341.6 1.2 collective-permute-start.10
  342.8 0.1 copy.8
  342.9 0.1 broadcast_in_dim.6
  343.0 0.1 reshape.33
  343.2 0.3 copy.9
  343.4 1.0 dynamic-slice_bitcast_fusion.1
  344.4 8.9 %visit.7 = f32[2,2,32,512]{3,2,1,0:T(8,128)} custom-call(bf16[2,32,12288]{2,1,0:T(8,128)(2,1)} %collective-permute-done.8.upper_ref, bf16[2,32,12288]{2,1,0:T(8,128)(2,1)} %collective-permute-done.9.lower_ref, bf16[512,32768]{1,0:T(8,128)(2,1)} %slab_ref.11), custom_call_target="tpu_custom_call" | custom-call | tf_op jit(solution)/shard_map/visit/pallas_call | solution.py:189
  353.3 0.4 collective-permute-start.18
  353.9 1.5 collective-permute-done.11.upper_ref
  355.4 28.9 %collective-permute-start.13 = (f32[96,512]{1,0:T(8,128)S(1)}, f32[96,512]{1,0:T(8,128)S(1)}, u32[]{:S(2)}, u32[]{:S(2)}) collective-permute-start(f32[96,512]{1,0:T(8,128)S(1)} %get-tuple-element.57), channel_id=1, source_target_pairs={{0,2},{2,4},{4,6},{6,8},{8,10},{10,12},{12,14},{14,16},{16,18},{18... | collective-permute-start | bytes 589832 | tf_op jit(solution)/shard_map/ppermute | solution.py:203
  384.3 8.8 %visit.8 = f32[2,2,32,512]{3,2,1,0:T(8,128)} custom-call(bf16[2,32,12288]{2,1,0:T(8,128)(2,1)} %collective-permute-done.11.upper_ref, bf16[2,32,12288]{2,1,0:T(8,128)(2,1)} %copy-done.2, bf16[512,32768]{1,0:T(8,128)(2,1)} %slab_ref.11), custom_call_target="tpu_custom_call" | custom-call | tf_op jit(solution)/shard_map/visit/pallas_call | solution.py:189
  393.2 6.4 %visit.9 = f32[2,2,32,512]{3,2,1,0:T(8,128)} custom-call(bf16[2,32,8192]{2,1,0:T(8,128)(2,1)} %collective-permute-done.14.upper_ref, bf16[2,32,8192]{2,1,0:T(8,128)(2,1)} %collective-permute-done.15.lower_ref, bf16[512,32768]{1,0:T(8,128)(2,1)} %slab_ref.11), custom_call_target="tpu_custom_call" | custom-call | tf_op jit(solution)/shard_map/visit/pallas_call | solution.py:189
  399.5 1.1 add_add_fusion
  400.7 19.7 %collective-permute-start.17 = (f32[32,512]{1,0:T(8,128)S(1)}, f32[32,512]{1,0:T(8,128)S(1)}, u32[]{:S(2)}, u32[]{:S(2)}) collective-permute-start(f32[32,512]{1,0:T(8,128)S(1)} %get-tuple-element.61), channel_id=1, source_target_pairs={{0,3},{1,2},{2,5},{3,4},{4,7},{5,6},{6,9},{7,8},{8,11},{9,10},{10,... | collective-permute-start | bytes 196616 | tf_op jit(solution)/shard_map/ppermute | solution.py:228
  420.3 14.2 %collective-permute-start.16 = (f32[32,512]{1,0:T(8,128)S(1)}, f32[32,512]{1,0:T(8,128)S(1)}, u32[]{:S(2)}, u32[]{:S(2)}) collective-permute-start(f32[32,512]{1,0:T(8,128)S(1)} %get-tuple-element.62), channel_id=1, source_target_pairs={{0,2},{1,3},{2,4},{3,5},{4,6},{5,7},{6,8},{7,9},{8,10},{9,11},{10,... | collective-permute-start | bytes 196616 | tf_op jit(solution)/shard_map/ppermute | solution.py:228
  434.6 0.1 collective-permute-start.20
  434.8 1.1 collective-permute-done.16
  435.9 13.5 %collective-permute-done.21 = f32[32,512]{1,0:T(8,128)S(1)} collective-permute-done((f32[32,512]{1,0:T(8,128)S(1)}, f32[32,512]{1,0:T(8,128)S(1)}, u32[]{:S(2)}, u32[]{:S(2)}) %collective-permute-start.21) | collective-permute-done | bytes 65568 | tf_op jit(solution)/shard_map/ppermute | solution.py:228
  449.4 0.6 collective-permute-done.20
  450.1 1.0 maximum_multiply_fusion
  (54 shorter events, 0.5 us)
Async XLA Ops:
  1.3 59.4 %collective-permute-start.1 = (bf16[2,8,32768]{2,1,0:T(8,128)(2,1)S(1)}, bf16[2,8,32768]{2,1,0:T(8,128)(2,1)S(1)}, u32[]{:S(2)}, u32[]{:S(2)}) collective-permute-start(bf16[2,8,32768]{2,1,0:T(8,128)(2,1)S(1)} %slice.44), channel_id=1, source_target_pairs={{0,2},{2,4},{4,6},{6,8},{8,10},{10,12},{12,14},{14,16},{16,18},{18... | collective-permute-start | bytes 3145736 | tf_op jit(solution)/shard_map/ppermute | solution.py:203
  4.0 59.3 %collective-permute-start = (bf16[2,8,32768]{2,1,0:T(8,128)(2,1)S(1)}, bf16[2,8,32768]{2,1,0:T(8,128)(2,1)}, u32[]{:S(2)}, u32[]{:S(2)}) collective-permute-start(bf16[2,8,32768]{2,1,0:T(8,128)(2,1)S(1)} %slice.44), channel_id=1, source_target_pairs={{0,30},{2,0},{4,2},{6,4},{8,6},{10,8},{12,10},{14,12},{16,14},{18,... | collective-permute-start | bytes 3145736 | tf_op jit(solution)/shard_map/ppermute | solution.py:203
  7.7 94.1 %collective-permute-start.5 = (bf16[2,24,32768]{2,1,0:T(8,128)(2,1)}, bf16[2,24,32768]{2,1,0:T(8,128)(2,1)}, u32[]{:S(2)}, u32[]{:S(2)}) collective-permute-start(bf16[2,24,32768]{2,1,0:T(8,128)(2,1)} %slice.45), channel_id=1, source_target_pairs={{0,2},{2,4},{4,6},{6,8},{8,10},{10,12},{12,14},{14,16},{16,18},{18... | collective-permute-start | bytes 9437192 | tf_op jit(solution)/shard_map/ppermute | solution.py:203
  9.5 154.9 %collective-permute-start.4 = (bf16[2,24,32768]{2,1,0:T(8,128)(2,1)}, bf16[2,24,32768]{2,1,0:T(8,128)(2,1)}, u32[]{:S(2)}, u32[]{:S(2)}) collective-permute-start(bf16[2,24,32768]{2,1,0:T(8,128)(2,1)} %slice.45), channel_id=1, source_target_pairs={{0,30},{2,0},{4,2},{6,4},{8,6},{10,8},{12,10},{14,12},{16,14},{18,... | collective-permute-start | bytes 9437192 | tf_op jit(solution)/shard_map/ppermute | solution.py:203
  60.7 1.0 copy-start.7
  100.8 105.5 %collective-permute-start.3 = (bf16[2,48,32768]{2,1,0:T(8,128)(2,1)}, bf16[2,48,32768]{2,1,0:T(8,128)(2,1)S(1)}, u32[]{:S(2)}, u32[]{:S(2)}) collective-permute-start(bf16[2,48,32768]{2,1,0:T(8,128)(2,1)} %get-tuple-element.32), channel_id=1, source_target_pairs={{0,2},{2,4},{4,6},{6,8},{8,10},{10,12},{12,14},{14,16},{16,18},{18... | collective-permute-start | bytes 18874376 | tf_op jit(solution)/shard_map/ppermute | solution.py:203
  101.8 169.3 %collective-permute-start.2 = (bf16[2,48,32768]{2,1,0:T(8,128)(2,1)}, bf16[2,48,32768]{2,1,0:T(8,128)(2,1)}, u32[]{:S(2)}, u32[]{:S(2)}) collective-permute-start(bf16[2,48,32768]{2,1,0:T(8,128)(2,1)} %get-tuple-element.32), channel_id=1, source_target_pairs={{0,30},{2,0},{4,2},{6,4},{8,6},{10,8},{12,10},{14,12},{16,14},{18,... | collective-permute-start | bytes 18874376 | tf_op jit(solution)/shard_map/ppermute | solution.py:203
  164.4 127.3 %collective-permute-start.7 = (bf16[2,16,32768]{2,1,0:T(8,128)(2,1)}, bf16[2,16,32768]{2,1,0:T(8,128)(2,1)}, u32[]{:S(2)}, u32[]{:S(2)}) collective-permute-start(bf16[2,16,32768]{2,1,0:T(8,128)(2,1)} %get-tuple-element.39), channel_id=1, source_target_pairs={{0,2},{2,4},{4,6},{6,8},{8,10},{10,12},{12,14},{14,16},{16,18},{18... | collective-permute-start | bytes 6291464 | tf_op jit(solution)/shard_map/ppermute | solution.py:203
  164.4 129.2 %collective-permute-start.6 = (bf16[2,16,32768]{2,1,0:T(8,128)(2,1)}, bf16[2,16,32768]{2,1,0:T(8,128)(2,1)}, u32[]{:S(2)}, u32[]{:S(2)}) collective-permute-start(bf16[2,16,32768]{2,1,0:T(8,128)(2,1)} %get-tuple-element.39), channel_id=1, source_target_pairs={{0,30},{2,0},{4,2},{6,4},{8,6},{10,8},{12,10},{14,12},{16,14},{18,... | collective-permute-start | bytes 6291464 | tf_op jit(solution)/shard_map/ppermute | solution.py:203
  206.4 65.3 %copy-start = (bf16[2,48,32768]{2,1,0:T(8,128)(2,1)}, bf16[2,48,32768]{2,1,0:T(8,128)(2,1)S(1)}, u32[]{:S(2)}) copy-start(bf16[2,48,32768]{2,1,0:T(8,128)(2,1)S(1)} %collective-permute-done.3.lower_ref) | copy-start | bytes 18874372
  271.1 43.0 %collective-permute-start.9 = (bf16[2,32,12288]{2,1,0:T(8,128)(2,1)S(1)}, bf16[2,32,12288]{2,1,0:T(8,128)(2,1)}, u32[]{:S(2)}, u32[]{:S(2)}) collective-permute-start(bf16[2,32,12288]{2,1,0:T(8,128)(2,1)S(1)} %get-tuple-element.43), channel_id=1, source_target_pairs={{0,2},{2,4},{4,6},{6,8},{8,10},{10,12},{12,14},{14,16},{16,18},{18... | collective-permute-start | bytes 4718600 | tf_op jit(solution)/shard_map/ppermute | solution.py:203
  271.1 67.4 %collective-permute-start.8 = (bf16[2,32,12288]{2,1,0:T(8,128)(2,1)S(1)}, bf16[2,32,12288]{2,1,0:T(8,128)(2,1)}, u32[]{:S(2)}, u32[]{:S(2)}) collective-permute-start(bf16[2,32,12288]{2,1,0:T(8,128)(2,1)S(1)} %get-tuple-element.43), channel_id=1, source_target_pairs={{0,30},{2,0},{4,2},{6,4},{8,6},{10,8},{12,10},{14,12},{16,14},{18,... | collective-permute-start | bytes 4718600 | tf_op jit(solution)/shard_map/ppermute | solution.py:203
  293.6 60.3 %collective-permute-start.12 = (bf16[2,32,12288]{2,1,0:T(8,128)(2,1)}, bf16[2,32,12288]{2,1,0:T(8,128)(2,1)S(1)}, u32[]{:S(2)}, u32[]{:S(2)}) collective-permute-start(bf16[2,32,12288]{2,1,0:T(8,128)(2,1)} %get-tuple-element.47), channel_id=1, source_target_pairs={{0,2},{2,4},{4,6},{6,8},{8,10},{10,12},{12,14},{14,16},{16,18},{18... | collective-permute-start | bytes 4718600 | tf_op jit(solution)/shard_map/ppermute | solution.py:203
  293.6 61.8 %collective-permute-start.11 = (bf16[2,32,12288]{2,1,0:T(8,128)(2,1)}, bf16[2,32,12288]{2,1,0:T(8,128)(2,1)}, u32[]{:S(2)}, u32[]{:S(2)}) collective-permute-start(bf16[2,32,12288]{2,1,0:T(8,128)(2,1)} %get-tuple-element.47), channel_id=1, source_target_pairs={{0,30},{2,0},{4,2},{6,4},{8,6},{10,8},{12,10},{14,12},{16,14},{18,... | collective-permute-start | bytes 4718600 | tf_op jit(solution)/shard_map/ppermute | solution.py:203
  296.3 17.8 %copy-start.1 = (f32[2,2,48,512]{3,2,1,0:T(8,128)S(1)}, f32[2,2,48,512]{3,2,1,0:T(8,128)}, u32[]{:S(2)}) copy-start(f32[2,2,48,512]{3,2,1,0:T(8,128)} %visit.5) | copy-start | bytes 1179652
  314.1 28.7 %copy-start.9 = (s32[8,24]{1,0:T(8,128)S(1)}, s32[8,24]{1,0:T(8,128)}, u32[]{:S(2)}) copy-start(s32[8,24]{1,0:T(8,128)} %param.9) | copy-start | bytes 2308
  338.5 54.6 %collective-permute-start.15 = (bf16[2,32,8192]{2,1,0:T(8,128)(2,1)}, bf16[2,32,8192]{2,1,0:T(8,128)(2,1)}, u32[]{:S(2)}, u32[]{:S(2)}) collective-permute-start(bf16[2,32,8192]{2,1,0:T(8,128)(2,1)} %slice.39), channel_id=1, source_target_pairs={{0,2},{2,4},{4,6},{6,8},{8,10},{10,12},{12,14},{14,16},{16,18},{18... | collective-permute-start | bytes 3145736 | tf_op jit(solution)/shard_map/ppermute | solution.py:203
  338.5 54.6 %collective-permute-start.14 = (bf16[2,32,8192]{2,1,0:T(8,128)(2,1)}, bf16[2,32,8192]{2,1,0:T(8,128)(2,1)}, u32[]{:S(2)}, u32[]{:S(2)}) collective-permute-start(bf16[2,32,8192]{2,1,0:T(8,128)(2,1)} %slice.39), channel_id=1, source_target_pairs={{0,30},{2,0},{4,2},{6,4},{8,6},{10,8},{12,10},{14,12},{16,14},{18,... | collective-permute-start | bytes 3145736 | tf_op jit(solution)/shard_map/ppermute | solution.py:203
  339.9 0.9 copy-start.3
  341.6 11.7 %collective-permute-start.10 = (f32[2,96,512]{2,1,0:T(8,128)}, f32[2,96,512]{2,1,0:T(8,128)S(1)}, u32[]{:S(2)}, u32[]{:S(2)}) collective-permute-start(f32[2,96,512]{2,1,0:T(8,128)} %dynamic-slice_bitcast_fusion), channel_id=1, source_target_pairs={{0,1},{1,0},{2,3},{3,2},{4,5},{5,4},{6,7},{7,6},{8,9},{9,8},{10,11... | collective-permute-start | bytes 1179656 | tf_op jit(solution)/shard_map/ppermute | solution.py:203
  344.4 9.4 %copy-start.4 = (f32[2,2,96,512]{3,2,1,0:T(8,128)S(1)}, f32[2,2,96,512]{3,2,1,0:T(8,128)}, u32[]{:S(2)}) copy-start(f32[2,2,96,512]{3,2,1,0:T(8,128)} %copy-done.3) | copy-start | bytes 2359300
  353.3 81.2 %collective-permute-start.18 = (f32[128,512]{1,0:T(8,128)S(1)}, f32[128,512]{1,0:T(8,128)S(1)}, u32[]{:S(2)}, u32[]{:S(2)}) collective-permute-start(f32[128,512]{1,0:T(8,128)S(1)} %dynamic-slice_bitcast_fusion.1), channel_id=1, source_target_pairs={{0,1},{1,0},{2,3},{3,2},{4,5},{5,4},{6,7},{7,6},{8,9},{9,8},{10,11... | collective-permute-start | bytes 786440 | tf_op jit(solution)/shard_map/ppermute | solution.py:203
  353.8 30.5 %copy-start.2 = (bf16[2,32,12288]{2,1,0:T(8,128)(2,1)}, bf16[2,32,12288]{2,1,0:T(8,128)(2,1)S(1)}, u32[]{:S(2)}) copy-start(bf16[2,32,12288]{2,1,0:T(8,128)(2,1)S(1)} %collective-permute-done.12.lower_ref) | copy-start | bytes 4718596
  355.4 94.6 %collective-permute-start.13 = (f32[96,512]{1,0:T(8,128)S(1)}, f32[96,512]{1,0:T(8,128)S(1)}, u32[]{:S(2)}, u32[]{:S(2)}) collective-permute-start(f32[96,512]{1,0:T(8,128)S(1)} %get-tuple-element.57), channel_id=1, source_target_pairs={{0,2},{2,4},{4,6},{6,8},{8,10},{10,12},{12,14},{14,16},{16,18},{18... | collective-permute-start | bytes 589832 | tf_op jit(solution)/shard_map/ppermute | solution.py:203
  384.3 65.8 %collective-permute-start.19 = (f32[96,512]{1,0:T(8,128)S(1)}, f32[96,512]{1,0:T(8,128)S(1)}, u32[]{:S(2)}, u32[]{:S(2)}) collective-permute-start(f32[96,512]{1,0:T(8,128)S(1)} %get-tuple-element.58), channel_id=1, source_target_pairs={{0,30},{2,0},{4,2},{6,4},{8,6},{10,8},{12,10},{14,12},{16,14},{18,... | collective-permute-start | bytes 589832 | tf_op jit(solution)/shard_map/ppermute | solution.py:203
  393.1 6.4 %copy-start.5 = (f32[2,2,32,512]{3,2,1,0:T(8,128)S(1)}, f32[2,2,32,512]{3,2,1,0:T(8,128)}, u32[]{:S(2)}) copy-start(f32[2,2,32,512]{3,2,1,0:T(8,128)} %visit.7) | copy-start | bytes 786436
  393.1 6.4 %copy-start.6 = (f32[2,2,32,512]{3,2,1,0:T(8,128)S(1)}, f32[2,2,32,512]{3,2,1,0:T(8,128)}, u32[]{:S(2)}) copy-start(f32[2,2,32,512]{3,2,1,0:T(8,128)} %visit.8) | copy-start | bytes 786436
  399.5 35.2 %copy-start.8 = (f32[2,128,512]{2,1,0:T(8,128)S(1)}, f32[2,128,512]{2,1,0:T(8,128)}, u32[]{:S(2)}) copy-start(f32[2,128,512]{2,1,0:T(8,128)} %get-tuple-element.54) | copy-start | bytes 1572868
  400.7 34.0 %collective-permute-start.17 = (f32[32,512]{1,0:T(8,128)S(1)}, f32[32,512]{1,0:T(8,128)S(1)}, u32[]{:S(2)}, u32[]{:S(2)}) collective-permute-start(f32[32,512]{1,0:T(8,128)S(1)} %get-tuple-element.61), channel_id=1, source_target_pairs={{0,3},{1,2},{2,5},{3,4},{4,7},{5,6},{6,9},{7,8},{8,11},{9,10},{10,... | collective-permute-start | bytes 196616 | tf_op jit(solution)/shard_map/ppermute | solution.py:228
  420.3 15.5 %collective-permute-start.16 = (f32[32,512]{1,0:T(8,128)S(1)}, f32[32,512]{1,0:T(8,128)S(1)}, u32[]{:S(2)}, u32[]{:S(2)}) collective-permute-start(f32[32,512]{1,0:T(8,128)S(1)} %get-tuple-element.62), channel_id=1, source_target_pairs={{0,2},{1,3},{2,4},{3,5},{4,6},{5,7},{6,8},{7,9},{8,10},{9,11},{10,... | collective-permute-start | bytes 196616 | tf_op jit(solution)/shard_map/ppermute | solution.py:228
  434.6 14.8 %collective-permute-start.21 = (f32[32,512]{1,0:T(8,128)S(1)}, f32[32,512]{1,0:T(8,128)S(1)}, u32[]{:S(2)}, u32[]{:S(2)}) collective-permute-start(f32[32,512]{1,0:T(8,128)S(1)} %get-tuple-element.63), channel_id=1, source_target_pairs={{0,31},{1,30},{2,1},{3,0},{4,3},{5,2},{6,5},{7,4},{8,7},{9,6},{10,... | collective-permute-start | bytes 196616 | tf_op jit(solution)/shard_map/ppermute | solution.py:228
  434.6 15.4 %collective-permute-start.20 = (f32[32,512]{1,0:T(8,128)S(1)}, f32[32,512]{1,0:T(8,128)S(1)}, u32[]{:S(2)}, u32[]{:S(2)}) collective-permute-start(f32[32,512]{1,0:T(8,128)S(1)} %get-tuple-element.64), channel_id=1, source_target_pairs={{0,30},{1,31},{2,0},{3,1},{4,2},{5,3},{6,4},{7,5},{8,6},{9,7},{10,... | collective-permute-start | bytes 196616 | tf_op jit(solution)/shard_map/ppermute | solution.py:228

commit v2 on v1

--- a/solution.py
+++ b/solution.py
@@ -9,10 +9,11 @@
 
 QB = 32
 SUB = 64
-CHUNKS = (1, 3, 6, 2, 4)
-PIECES = (3, 3, 2)
+CHUNKS = (2, 10, 4)
+PIECES = (4, 2, 2)
 WIDE = 256
 LOW = 8
+LANES = 128
 VMEM = 56 * 1024 * 1024
 NT = (((1,), (1,)), ((), ()))
 TN = (((0,), (0,)), ((), ()))
@@ -129,7 +130,7 @@
 
 def visit_raw_kernel(count, *refs):
     pieces = refs[:count]
-    in_ref, out_ref, slab_ref, scores_ref, turned, left, held = refs[count:]
+    in_ref, out_ref, slab_ref, _, scores_ref, turned, left, held = refs[count:]
     _, groups, rows, _ = scores_ref.shape
     at = 0
     for piece in pieces:
@@ -142,7 +143,7 @@
     add_scores(held[...], slab_ref[...], scores_ref)
 
 
-def visit_raw(raw, inv_in, inv_out, store):
+def visit_raw(raw, inv_in, inv_out, store, word):
     modules, side, _ = inv_in.shape
     size = side * side
     examples = store.shape[0]
@@ -155,7 +156,8 @@
         functools.partial(visit_raw_kernel, len(pieces)),
         grid=(modules,),
         in_specs=[pl.BlockSpec((*p.shape[:2], size), lambda m: (0, 0, m)) for p in pieces]
-        + [small, small, pl.BlockSpec((examples, size), lambda m: (0, m))],
+        + [small, small, pl.BlockSpec((examples, size), lambda m: (0, m))]
+        + [pl.BlockSpec(memory_space=pl.ANY)],
         out_specs=pl.BlockSpec((2, groups, sum(counts), examples), lambda m: (0, 0, 0, 0)),
         out_shape=jax.ShapeDtypeStruct((2, groups, sum(counts), examples), jnp.float32),
         scratch_shapes=[
@@ -165,7 +167,7 @@
         ],
         compiler_params=pltpu.CompilerParams(vmem_limit_bytes=VMEM),
         name="visit_raw",
-    )(*pieces, inv_in, inv_out, store)
+    )(*pieces, inv_in, inv_out, store, word)
     flat = scores.reshape(2, -1, examples)
     at, found = 0, []
     for count in counts:
@@ -174,7 +176,7 @@
     return jnp.concatenate(found, axis=2)
 
 
-def visit_kernel(upper_ref, lower_ref, slab_ref, scores_ref):
+def visit_kernel(upper_ref, lower_ref, slab_ref, _, scores_ref):
     groups, rows, width = upper_ref.shape
     both = jnp.concatenate(
         [upper_ref[...].reshape(groups * rows, width), lower_ref[...].reshape(groups * rows, width)]
@@ -182,19 +184,24 @@
     add_scores(both, slab_ref[...], scores_ref)
 
 
-def visit(upper, lower, store, first, unit):
+def visit(upper, lower, store, first, unit, word):
     groups, rows, width = upper.shape
     examples = store.shape[0]
     block = pl.BlockSpec((groups, rows, unit), lambda s: (0, 0, s))
     return pl.pallas_call(
         visit_kernel,
         grid=(width // unit,),
-        in_specs=[block, block, pl.BlockSpec((examples, unit), lambda s: (0, s + first))],
+        in_specs=[
+            block,
+            block,
+            pl.BlockSpec((examples, unit), lambda s: (0, s + first)),
+            pl.BlockSpec(memory_space=pl.ANY),
+        ],
         out_specs=pl.BlockSpec((2, groups, rows, examples), lambda s: (0, 0, 0, 0)),
         out_shape=jax.ShapeDtypeStruct((2, groups, rows, examples), jnp.float32),
         compiler_params=pltpu.CompilerParams(vmem_limit_bytes=VMEM),
         name="visit",
-    )(upper, lower, store)
+    )(upper, lower, store, word)
 
 
 def shifted(value, axis, steps):
@@ -244,37 +251,40 @@
         return shifted(value, "ex", -1), shifted(value, "ex", 1)
 
     split = queries.reshape(groups, rows, dims)
-    first = lax.optimization_barrier(split[:, : bounds[1]])
-    raw_one = send(first)
-    raw_two = send(split[:, bounds[1] : bounds[2]])
-    queries, raw_one = together((queries, raw_one))
-    (a, b, c), mine = own(queries, inv_in, inv_out, store, groups, bounds[2:])
+    first, queries = together((split[:, : bounds[1]], queries))
+    came_raw = send(first)
+    (a, c), mine = own(queries, inv_in, inv_out, store, groups, bounds[1:])
     cuts = []
     start = 0
     for count in PIECES:
         cuts.append(c[..., start * unit : (start + count) * unit])
         start += count
 
+    def both_there(came, work):
+        word, came, work = together((came[0][0, :, :LANES], came, work))
+        pairs = [(i, i ^ 1) for i in range(lax.axis_size("ex"))]
+        return lax.ppermute(word, "ex", pairs), came, work
+
+    word, came_raw, mine = both_there(came_raw, mine)
+    a, cut, word = together((a, cuts[0], word))
     came_a = send(a)
-    b, raw_two = together((b, raw_two))
-    came_b = send(b)
-    scores_raw = visit_raw([raw_one, raw_two], inv_in, inv_out, store)
-    cut, came_a, scores_raw = together((cuts[0], came_a, scores_raw))
     came_c = [send(cut)]
-    scores_a = visit(*came_a, store, 0, unit)
-    cut, came_b, scores_a = together((cuts[1], came_b, scores_a))
+    scores_raw = visit_raw([came_raw], inv_in, inv_out, store, word)
+    own_scores = grp_sum(mine, 0)
+    word, came_a, (scores_raw, own_scores) = both_there(came_a, (scores_raw, own_scores))
+    cut, word = together((cuts[1], word))
     came_c.append(send(cut))
-    scores_b = visit(*came_b, store, 0, unit)
-    cut, came_c[0], scores_b = together((cuts[2], came_c[0], scores_b))
+    scores_a = visit(*came_a, store, 0, unit, word)
+    both = grp_sum(jnp.concatenate([scores_raw, scores_a], axis=2), 1)
+    word, came_c[0], both = both_there(came_c[0], both)
+    cut, word = together((cuts[2], word))
     came_c.append(send(cut))
-    both = grp_sum(jnp.concatenate([scores_raw, scores_a, scores_b], axis=2), 1)
-    part = visit(*came_c[0], store, 0, unit)
+    part = visit(*came_c[0], store, 0, unit, word)
     both, came_c[1] = together((both, came_c[1]))
     upper_scores = [shifted(both[0], "ex", 1)]
     lower_scores = [shifted(both[1], "ex", -1)]
-    part = part + visit(*came_c[1], store, PIECES[0], unit)
-    own_scores = grp_sum(mine, 0)
-    part = part + visit(*came_c[2], store, PIECES[0] + PIECES[1], unit)
+    part = part + visit(*came_c[1], store, PIECES[0], unit, word)
+    part = part + visit(*came_c[2], store, PIECES[0] + PIECES[1], unit, word)
     upper_scores.append(to_owner(part[0], 1))
     lower_scores.append(to_owner(part[1], -1))
 

time: 458 us -> 401 us (0.88); the launches traced: 451 us -> 400 us
  starting transfers between devices: 73.2 us -> 21.9 us
  waiting for transfers between devices: 222 us -> 241 us
  Pallas kernels: 136 us -> 118 us
    ppermute x18 -> x14, waiting for transfers between devices: 207 us -> 238 us  [shifted(): return lax.ppermute(value, axis, pairs)]
    ppermute x4, starting transfers between devices: 34 us -> 5.51 us  [to_owner(): arrived = lax.ppermute(share, ('ex', 'grp'), pairs)]
    ppermute x18 -> x14, starting transfers between devices: 39.2 us -> 15 us  [shifted(): return lax.ppermute(value, axis, pairs)]
    pallas_call x5 -> x4, Pallas kernels: 61.9 us -> 45.1 us  [visit(): pl.pallas_call(visit_kernel, grid=(width // unit,), in_specs=[block, bloc...]
    ppermute x4, waiting for transfers between devices: 15.3 us -> 2.27 us  [to_owner(): arrived = lax.ppermute(share, ('ex', 'grp'), pairs)]
  transfers between devices with their start and end apart: 22 -> 21, of which waited for: 10 -> 8; matrix products, arithmetic and copies ran while one was open for 3% -> 3% of each run, Pallas kernels for 30% -> 30%
where the time goes in v2:
time: 401 us; the launch traced here: 400 us
  waiting for transfers between devices  241 us (60%)
  Pallas kernels  118 us (29%)
  starting transfers between devices  21.9 us (5%)
  local copies, waits for them, and re-layouts  13.8 us (3%)
  other arithmetic  4.9 us (1%)
    ppermute x14, waiting for transfers between devices, shifted(): return lax.ppermute(value, axis, pairs)  238 us
    pallas_call x4, Pallas kernels, visit(): pl.pallas_call(visit_kernel, grid=(width // unit,), in_specs=[block, bloc...  45.1 us
    pallas_call x1, Pallas kernels, own(): pl.pallas_call(functools.partial(own_kernel, bounds), grid=(modules,), in...  37.7 us
    pallas_call x1, Pallas kernels, visit_raw(): pl.pallas_call(functools.partial(visit_raw_kernel, len(pieces)), grid=(mo...  35.3 us
    ppermute x14, starting transfers between devices, shifted(): return lax.ppermute(value, axis, pairs)  15 us
  transfers between devices with their start and end apart: 21, of which 8 were waited for; matrix products, arithmetic and copies ran while one was open for 3% of the time, Pallas kernels for 30%

profile of v2, /device:TPU:1, one launch (start us, length us, event | category | flops | bytes accessed | tf_op | source)
XLA Modules:
  0.0 399.6 jit_solution(7779601025513947927)
XLA Ops:
  0.0 1.7 slice.44
  1.7 0.1 collective-permute-start
  1.8 2.6 collective-permute-start.1
  4.5 37.7 %own.1 = (bf16[2,80,32768]{2,1,0:T(8,128)(2,1)}, bf16[2,32,32768]{2,1,0:T(8,128)(2,1)}, f32[2,128,512]{2,1,0:T(8,128)}) custom-call(bf16[256,32768]{1,0:T(8,128)(2,1)} %x_ref, bf16[8,64,64]{2,1,0:T(8,128)(2,1)} %refs_2_.1, bf16[8,64,64]{2,1,0:T(8,128)(2,1)} %refs_3_.1, bf16[512,32768]{1,0:T(8,128)(2,1)} %slab_ref.9), custom_call_target="tpu_custom_call" | custom-call | tf_op jit(solution)/shard_map/own/pallas_call | solution.py:107
  42.2 8.4 %collective-permute-done.refs_0_ = bf16[2,16,32768]{2,1,0:T(8,128)(2,1)S(1)} collective-permute-done((bf16[2,16,32768]{2,1,0:T(8,128)(2,1)S(1)}, bf16[2,16,32768]{2,1,0:T(8,128)(2,1)S(1)}, u32[]{:S(2)}, u32[]{:S(2)}) %collective-permute-start) | collective-permute-done | bytes 2097184 | tf_op jit(solution)/shard_map/ppermute | solution.py:210
  50.6 1.4 copy-done.2
  52.0 3.0 slice.34
  55.0 0.5 collective-permute-start.5
  55.5 1.2 collective-permute-start.6
  56.8 1.3 collective-permute-start.7
  58.1 2.6 collective-permute-start.3
  60.7 35.3 %visit_raw.1 = f32[2,2,16,512]{3,2,1,0:T(8,128)} custom-call(bf16[2,16,32768]{2,1,0:T(8,128)(2,1)} %copy-done.2, bf16[2,16,32768]{2,1,0:T(8,128)(2,1)} %collective-permute-done.1.refs_1_, bf16[8,64,64]{2,1,0:T(8,128)(2,1)} %refs_2_.1, bf16[8,64,64]{2,1,0:T(8,128)(2,1)} %refs_3_.1, bf16[512,32768]{1,0:T(8,128)(2,1)} %slab_ref.9, bf16[16,128]{1,0:T(8,128)(2,1)} %copy-done.12), custom_call_target="tpu_custom_call" | custom-call | tf_op jit(solution)/shard_map/visit_raw/pallas_call | solution.py:155
  96.0 0.7 bitcast_add_fusion
  96.7 208.8 %collective-permute-done.5.upper_ref = bf16[2,80,32768]{2,1,0:T(8,128)(2,1)} collective-permute-done((bf16[2,80,32768]{2,1,0:T(8,128)(2,1)}, bf16[2,80,32768]{2,1,0:T(8,128)(2,1)}, u32[]{:S(2)}, u32[]{:S(2)}) %collective-permute-start.5) | collective-permute-done | bytes 10485792 | tf_op jit(solution)/shard_map/ppermute | solution.py:210
  305.5 0.7 slice_bitcast_fusion.2
  306.3 1.5 fusion.5
  307.7 0.6 copy-done.11
  308.3 21.8 %visit.4 = f32[2,2,80,512]{3,2,1,0:T(8,128)} custom-call(bf16[2,80,32768]{2,1,0:T(8,128)(2,1)} %collective-permute-done.5.upper_ref, bf16[2,80,32768]{2,1,0:T(8,128)(2,1)} %collective-permute-done.6.lower_ref, bf16[512,32768]{1,0:T(8,128)(2,1)} %slab_ref.9, bf16[80,128]{1,0:T(8,128)(2,1)} %copy-done.11), custom_call_target="tpu_custom_call" | custom-call | tf_op jit(solution)/shard_map/visit/pallas_call | solution.py:191
  330.1 1.0 fusion.1
  331.1 1.3 collective-permute-start.9
  332.4 0.8 collective-permute-start.10
  333.3 1.0 collective-permute-start.11
  334.2 7.2 %collective-permute-done.9 = f32[2,96,512]{2,1,0:T(8,128)S(1)} collective-permute-done((f32[2,96,512]{2,1,0:T(8,128)S(1)}, f32[2,96,512]{2,1,0:T(8,128)S(1)}, u32[]{:S(2)}, u32[]{:S(2)}) %collective-permute-start.9) | collective-permute-done | bytes 393248 | tf_op jit(solution)/shard_map/ppermute | solution.py:210
  341.4 1.0 fusion.4
  342.4 1.4 collective-permute-start.13
  343.8 0.8 collective-permute-done.13._
  344.7 0.3 collective-permute-start.14
  345.0 1.4 collective-permute-start.15
  346.4 0.7 copy.8
  347.1 1.4 broadcast_in_dim.6
  348.5 1.6 reshape.21
  350.1 10.6 %visit.5 = f32[2,2,32,512]{3,2,1,0:T(8,128)} custom-call(bf16[2,32,16384]{2,1,0:T(8,128)(2,1)} %copy-done.1, bf16[2,32,16384]{2,1,0:T(8,128)(2,1)} %collective-permute-done.4.lower_ref, bf16[512,32768]{1,0:T(8,128)(2,1)} %slab_ref.9, bf16[32,128]{1,0:T(8,128)(2,1)} %copy-done.9), custom_call_target="tpu_custom_call" | custom-call | tf_op jit(solution)/shard_map/visit/pallas_call | solution.py:191
  360.8 8.6 %collective-permute-done.10.upper_ref = bf16[2,32,8192]{2,1,0:T(8,128)(2,1)S(1)} collective-permute-done((bf16[2,32,8192]{2,1,0:T(8,128)(2,1)}, bf16[2,32,8192]{2,1,0:T(8,128)(2,1)S(1)}, u32[]{:S(2)}, u32[]{:S(2)}) %collective-permute-start.10) | collective-permute-done | bytes 1048608 | tf_op jit(solution)/shard_map/ppermute | solution.py:210
  369.4 0.8 slice_bitcast_fusion.1
  370.1 1.8 collective-permute-start.12
  372.0 6.3 %visit.6 = f32[2,2,32,512]{3,2,1,0:T(8,128)} custom-call(bf16[2,32,8192]{2,1,0:T(8,128)(2,1)} %copy-done.5, bf16[2,32,8192]{2,1,0:T(8,128)(2,1)} %collective-permute-done.11.lower_ref, bf16[512,32768]{1,0:T(8,128)(2,1)} %slab_ref.9, bf16[32,128]{1,0:T(8,128)(2,1)} %copy-done.9), custom_call_target="tpu_custom_call" | custom-call | tf_op jit(solution)/shard_map/visit/pallas_call | solution.py:191
  378.3 4.6 %collective-permute-done.14.upper_ref = bf16[2,32,8192]{2,1,0:T(8,128)(2,1)} collective-permute-done((bf16[2,32,8192]{2,1,0:T(8,128)(2,1)}, bf16[2,32,8192]{2,1,0:T(8,128)(2,1)}, u32[]{:S(2)}, u32[]{:S(2)}) %collective-permute-start.14) | collective-permute-done | bytes 1048608 | tf_op jit(solution)/shard_map/ppermute | solution.py:210
  382.8 6.3 %visit.7 = f32[2,2,32,512]{3,2,1,0:T(8,128)} custom-call(bf16[2,32,8192]{2,1,0:T(8,128)(2,1)} %collective-permute-done.14.upper_ref, bf16[2,32,8192]{2,1,0:T(8,128)(2,1)} %collective-permute-done.15.lower_ref, bf16[512,32768]{1,0:T(8,128)(2,1)} %slab_ref.9, bf16[32,128]{1,0:T(8,128)(2,1)} %copy-done.9), custom_call_target="tpu_custom_call" | custom-call | tf_op jit(solution)/shard_map/visit/pallas_call | solution.py:191
  389.2 1.1 add_add_fusion
  390.3 1.8 collective-permute-start.16
  392.1 0.0 collective-permute-start.17
  392.1 0.7 collective-permute-start.19
  392.8 0.6 collective-permute-done.16
  393.4 3.0 collective-permute-start.20
  396.4 0.1 broadcast_in_dim.7
  396.5 0.3 copy.9
  396.8 1.6 collective-permute-done.20
  398.6 1.0 maximum_multiply_fusion
  (55 shorter events, 0.2 us)
Async XLA Ops:
  1.7 48.9 %collective-permute-start = (bf16[2,16,32768]{2,1,0:T(8,128)(2,1)S(1)}, bf16[2,16,32768]{2,1,0:T(8,128)(2,1)S(1)}, u32[]{:S(2)}, u32[]{:S(2)}) collective-permute-start(bf16[2,16,32768]{2,1,0:T(8,128)(2,1)S(1)} %slice.44), channel_id=1, source_target_pairs={{0,30},{2,0},{4,2},{6,4},{8,6},{10,8},{12,10},{14,12},{16,14},{18,... | collective-permute-start | bytes 6291464 | tf_op jit(solution)/shard_map/ppermute | solution.py:210
  1.8 50.1 %collective-permute-start.1 = (bf16[2,16,32768]{2,1,0:T(8,128)(2,1)S(1)}, bf16[2,16,32768]{2,1,0:T(8,128)(2,1)}, u32[]{:S(2)}, u32[]{:S(2)}) collective-permute-start(bf16[2,16,32768]{2,1,0:T(8,128)(2,1)S(1)} %slice.44), channel_id=1, source_target_pairs={{0,2},{2,4},{4,6},{6,8},{8,10},{10,12},{12,14},{14,16},{16,18},{18... | collective-permute-start | bytes 6291464 | tf_op jit(solution)/shard_map/ppermute | solution.py:210
  42.2 14.6 %copy-start.8 = (f32[2,128,512]{2,1,0:T(8,128)S(1)}, f32[2,128,512]{2,1,0:T(8,128)}, u32[]{:S(2)}) copy-start(f32[2,128,512]{2,1,0:T(8,128)} %get-tuple-element.44) | copy-start | bytes 1572868
  50.6 1.4 copy-start.2
  52.0 3.1 collective-permute-start.2
  55.0 5.7 %copy-start.12 = (bf16[16,128]{1,0:T(8,128)(2,1)}, bf16[16,128]{1,0:T(8,128)(2,1)S(1)}, u32[]{:S(2)}) copy-start(bf16[16,128]{1,0:T(8,128)(2,1)S(1)} %collective-permute-done.2.refs_5_) | copy-start | bytes 12292
  55.0 250.5 %collective-permute-start.5 = (bf16[2,80,32768]{2,1,0:T(8,128)(2,1)}, bf16[2,80,32768]{2,1,0:T(8,128)(2,1)}, u32[]{:S(2)}, u32[]{:S(2)}) collective-permute-start(bf16[2,80,32768]{2,1,0:T(8,128)(2,1)} %get-tuple-element.40), channel_id=1, source_target_pairs={{0,30},{2,0},{4,2},{6,4},{8,6},{10,8},{12,10},{14,12},{16,14},{18,... | collective-permute-start | bytes 31457288 | tf_op jit(solution)/shard_map/ppermute | solution.py:210
  55.5 250.7 %collective-permute-start.6 = (bf16[2,80,32768]{2,1,0:T(8,128)(2,1)}, bf16[2,80,32768]{2,1,0:T(8,128)(2,1)}, u32[]{:S(2)}, u32[]{:S(2)}) collective-permute-start(bf16[2,80,32768]{2,1,0:T(8,128)(2,1)} %get-tuple-element.40), channel_id=1, source_target_pairs={{0,2},{2,4},{4,6},{6,8},{8,10},{10,12},{12,14},{14,16},{16,18},{18... | collective-permute-start | bytes 31457288 | tf_op jit(solution)/shard_map/ppermute | solution.py:210
  56.8 39.2 %collective-permute-start.7 = (f32[128,512]{1,0:T(8,128)S(1)}, f32[128,512]{1,0:T(8,128)S(1)}, u32[]{:S(2)}, u32[]{:S(2)}) collective-permute-start(f32[128,512]{1,0:T(8,128)S(1)} %dynamic-slice_bitcast_fusion), channel_id=1, source_target_pairs={{0,1},{1,0},{2,3},{3,2},{4,5},{5,4},{6,7},{7,6},{8,9},{9,8},{10,11... | collective-permute-start | bytes 786440 | tf_op jit(solution)/shard_map/ppermute | solution.py:210
  58.1 248.2 %copy-start = (bf16[2,32,32768]{2,1,0:T(8,128)(2,1)S(1)}, bf16[2,32,32768]{2,1,0:T(8,128)(2,1)}, u32[]{:S(2)}) copy-start(bf16[2,32,32768]{2,1,0:T(8,128)(2,1)} %get-tuple-element.35) | copy-start | bytes 12582916
  58.1 274.3 %collective-permute-start.3 = (bf16[2,32,16384]{2,1,0:T(8,128)(2,1)}, bf16[2,32,16384]{2,1,0:T(8,128)(2,1)S(1)}, u32[]{:S(2)}, u32[]{:S(2)}) collective-permute-start(bf16[2,32,16384]{2,1,0:T(8,128)(2,1)} %slice.34), channel_id=1, source_target_pairs={{0,30},{2,0},{4,2},{6,4},{8,6},{10,8},{12,10},{14,12},{16,14},{18,... | collective-permute-start | bytes 6291464 | tf_op jit(solution)/shard_map/ppermute | solution.py:210
  60.7 281.7 %collective-permute-start.4 = (bf16[2,32,16384]{2,1,0:T(8,128)(2,1)}, bf16[2,32,16384]{2,1,0:T(8,128)(2,1)}, u32[]{:S(2)}, u32[]{:S(2)}) collective-permute-start(bf16[2,32,16384]{2,1,0:T(8,128)(2,1)} %slice.34), channel_id=1, source_target_pairs={{0,2},{2,4},{4,6},{6,8},{8,10},{10,12},{12,14},{14,16},{16,18},{18... | collective-permute-start | bytes 6291464 | tf_op jit(solution)/shard_map/ppermute | solution.py:210
  306.2 1.5 collective-permute-start.8
  307.7 0.6 copy-start.11
  308.3 21.8 %copy-start.3 = (f32[2,2,16,512]{3,2,1,0:T(8,128)S(1)}, f32[2,2,16,512]{3,2,1,0:T(8,128)}, u32[]{:S(2)}) copy-start(f32[2,2,16,512]{3,2,1,0:T(8,128)} %visit_raw.1) | copy-start | bytes 393220
  308.3 38.1 %copy-start.13 = (s32[8,24]{1,0:T(8,128)S(1)}, s32[8,24]{1,0:T(8,128)}, u32[]{:S(2)}) copy-start(s32[8,24]{1,0:T(8,128)} %param.9) | copy-start | bytes 2308
  331.1 10.2 %collective-permute-start.9 = (f32[2,96,512]{2,1,0:T(8,128)S(1)}, f32[2,96,512]{2,1,0:T(8,128)S(1)}, u32[]{:S(2)}, u32[]{:S(2)}) collective-permute-start(f32[2,96,512]{2,1,0:T(8,128)S(1)} %fusion.1), channel_id=1, source_target_pairs={{0,1},{1,0},{2,3},{3,2},{4,5},{5,4},{6,7},{7,6},{8,9},{9,8},{10,11... | collective-permute-start | bytes 1179656 | tf_op jit(solution)/shard_map/ppermute | solution.py:210
  332.4 17.7 %copy-start.1 = (bf16[2,32,16384]{2,1,0:T(8,128)(2,1)}, bf16[2,32,16384]{2,1,0:T(8,128)(2,1)S(1)}, u32[]{:S(2)}) copy-start(bf16[2,32,16384]{2,1,0:T(8,128)(2,1)S(1)} %collective-permute-done.3.upper_ref) | copy-start | bytes 6291460
  332.4 37.0 %collective-permute-start.10 = (bf16[2,32,8192]{2,1,0:T(8,128)(2,1)}, bf16[2,32,8192]{2,1,0:T(8,128)(2,1)S(1)}, u32[]{:S(2)}, u32[]{:S(2)}) collective-permute-start(bf16[2,32,8192]{2,1,0:T(8,128)(2,1)} %get-tuple-element.51), channel_id=1, source_target_pairs={{0,30},{2,0},{4,2},{6,4},{8,6},{10,8},{12,10},{14,12},{16,14},{18,... | collective-permute-start | bytes 3145736 | tf_op jit(solution)/shard_map/ppermute | solution.py:210
  333.3 36.1 %collective-permute-start.11 = (bf16[2,32,8192]{2,1,0:T(8,128)(2,1)}, bf16[2,32,8192]{2,1,0:T(8,128)(2,1)}, u32[]{:S(2)}, u32[]{:S(2)}) collective-permute-start(bf16[2,32,8192]{2,1,0:T(8,128)(2,1)} %get-tuple-element.51), channel_id=1, source_target_pairs={{0,2},{2,4},{4,6},{6,8},{8,10},{10,12},{12,14},{14,16},{16,18},{18... | collective-permute-start | bytes 3145736 | tf_op jit(solution)/shard_map/ppermute | solution.py:210
  342.4 2.2 collective-permute-start.13
  344.7 5.5 %copy-start.9 = (bf16[32,128]{1,0:T(8,128)(2,1)}, bf16[32,128]{1,0:T(8,128)(2,1)S(1)}, u32[]{:S(2)}) copy-start(bf16[32,128]{1,0:T(8,128)(2,1)S(1)} %collective-permute-done.13._) | copy-start | bytes 24580
  344.7 38.2 %collective-permute-start.14 = (bf16[2,32,8192]{2,1,0:T(8,128)(2,1)}, bf16[2,32,8192]{2,1,0:T(8,128)(2,1)}, u32[]{:S(2)}, u32[]{:S(2)}) collective-permute-start(bf16[2,32,8192]{2,1,0:T(8,128)(2,1)} %get-tuple-element.59), channel_id=1, source_target_pairs={{0,30},{2,0},{4,2},{6,4},{8,6},{10,8},{12,10},{14,12},{16,14},{18,... | collective-permute-start | bytes 3145736 | tf_op jit(solution)/shard_map/ppermute | solution.py:210
  345.0 37.8 %collective-permute-start.15 = (bf16[2,32,8192]{2,1,0:T(8,128)(2,1)}, bf16[2,32,8192]{2,1,0:T(8,128)(2,1)}, u32[]{:S(2)}, u32[]{:S(2)}) collective-permute-start(bf16[2,32,8192]{2,1,0:T(8,128)(2,1)} %get-tuple-element.59), channel_id=1, source_target_pairs={{0,2},{2,4},{4,6},{6,8},{8,10},{10,12},{12,14},{14,16},{16,18},{18... | collective-permute-start | bytes 3145736 | tf_op jit(solution)/shard_map/ppermute | solution.py:210
  369.4 2.6 copy-start.5
  370.1 28.3 %collective-permute-start.12 = (f32[96,512]{1,0:T(8,128)}, f32[96,512]{1,0:T(8,128)S(1)}, u32[]{:S(2)}, u32[]{:S(2)}) collective-permute-start(f32[96,512]{1,0:T(8,128)} %get-tuple-element.63), channel_id=1, source_target_pairs={{0,2},{2,4},{4,6},{6,8},{8,10},{10,12},{12,14},{14,16},{16,18},{18... | collective-permute-start | bytes 589832 | tf_op jit(solution)/shard_map/ppermute | solution.py:210
  371.9 26.6 %collective-permute-start.18 = (f32[96,512]{1,0:T(8,128)S(1)}, f32[96,512]{1,0:T(8,128)S(1)}, u32[]{:S(2)}, u32[]{:S(2)}) collective-permute-start(f32[96,512]{1,0:T(8,128)S(1)} %get-tuple-element.64), channel_id=1, source_target_pairs={{0,30},{2,0},{4,2},{6,4},{8,6},{10,8},{12,10},{14,12},{16,14},{18,... | collective-permute-start | bytes 589832 | tf_op jit(solution)/shard_map/ppermute | solution.py:210
  378.3 10.9 %copy-start.4 = (f32[2,2,32,512]{3,2,1,0:T(8,128)S(1)}, f32[2,2,32,512]{3,2,1,0:T(8,128)}, u32[]{:S(2)}) copy-start(f32[2,2,32,512]{3,2,1,0:T(8,128)} %visit.6) | copy-start | bytes 786436
  378.3 10.9 %copy-start.7 = (f32[2,2,32,512]{3,2,1,0:T(8,128)S(1)}, f32[2,2,32,512]{3,2,1,0:T(8,128)}, u32[]{:S(2)}) copy-start(f32[2,2,32,512]{3,2,1,0:T(8,128)} %visit.5) | copy-start | bytes 786436
  378.3 18.2 %copy-start.10 = (f32[256,24]{0,1:T(8,128)S(1)}, f32[256,24]{0,1:T(8,128)}, u32[]{:S(2)}) copy-start(f32[256,24]{0,1:T(8,128)} %reshape.21) | copy-start | bytes 73732
  389.2 9.4 %copy-start.6 = (f32[128,512]{1,0:T(8,128)S(1)}, f32[128,512]{1,0:T(8,128)}, u32[]{:S(2)}) copy-start(f32[128,512]{1,0:T(8,128)} %bitcast_add_fusion) | copy-start | bytes 786436
  390.3 3.1 collective-permute-start.16
  392.1 4.7 %collective-permute-start.17 = (f32[32,512]{1,0:T(8,128)S(1)}, f32[32,512]{1,0:T(8,128)S(1)}, u32[]{:S(2)}, u32[]{:S(2)}) collective-permute-start(f32[32,512]{1,0:T(8,128)S(1)} %get-tuple-element.67), channel_id=1, source_target_pairs={{0,3},{1,2},{2,5},{3,4},{4,7},{5,6},{6,9},{7,8},{8,11},{9,10},{10,... | collective-permute-start | bytes 196616 | tf_op jit(solution)/shard_map/ppermute | solution.py:235
  392.1 4.7 %collective-permute-start.19 = (f32[32,512]{1,0:T(8,128)S(1)}, f32[32,512]{1,0:T(8,128)S(1)}, u32[]{:S(2)}, u32[]{:S(2)}) collective-permute-start(f32[32,512]{1,0:T(8,128)S(1)} %get-tuple-element.70), channel_id=1, source_target_pairs={{0,30},{1,31},{2,0},{3,1},{4,2},{5,3},{6,4},{7,5},{8,6},{9,7},{10,... | collective-permute-start | bytes 196616 | tf_op jit(solution)/shard_map/ppermute | solution.py:235
  393.4 5.0 %collective-permute-start.20 = (f32[32,512]{1,0:T(8,128)S(1)}, f32[32,512]{1,0:T(8,128)S(1)}, u32[]{:S(2)}, u32[]{:S(2)}) collective-permute-start(f32[32,512]{1,0:T(8,128)S(1)} %get-tuple-element.69), channel_id=1, source_target_pairs={{0,31},{1,30},{2,1},{3,0},{4,3},{5,2},{6,5},{7,4},{8,7},{9,6},{10,... | collective-permute-start | bytes 196616 | tf_op jit(solution)/shard_map/ppermute | solution.py:235

commit v3 on v2

--- a/solution.py
+++ b/solution.py
@@ -10,7 +10,7 @@
 QB = 32
 SUB = 64
 CHUNKS = (2, 10, 4)
-PIECES = (4, 2, 2)
+PIECES = (4, 3, 1)
 WIDE = 256
 LOW = 8
 LANES = 128
@@ -70,12 +70,13 @@
     return blocks
 
 
-def add_scores(rows, slab, out_ref):
+def add_scores(rows, slab, out_ref, base=None):
     part = lax.dot_general(rows, slab, NT, preferred_element_type=jnp.float32)
 
     @pl.when(pl.program_id(0) == 0)
     def _():
-        out_ref[...] = part.reshape(out_ref.shape)
+        first = part.reshape(out_ref.shape)
+        out_ref[...] = first if base is None else base[...] + first
 
     @pl.when(pl.program_id(0) != 0)
     def _():
@@ -176,32 +177,35 @@
     return jnp.concatenate(found, axis=2)
 
 
-def visit_kernel(upper_ref, lower_ref, slab_ref, _, scores_ref):
+def visit_kernel(count, upper_ref, lower_ref, slab_ref, *rest):
+    *base, scores_ref = rest[count:]
     groups, rows, width = upper_ref.shape
     both = jnp.concatenate(
         [upper_ref[...].reshape(groups * rows, width), lower_ref[...].reshape(groups * rows, width)]
     )
-    add_scores(both, slab_ref[...], scores_ref)
-
-
-def visit(upper, lower, store, first, unit, word):
+    add_scores(both, slab_ref[...], scores_ref, *base)
+
+
+def visit(upper, lower, store, first, unit, words, *base):
     groups, rows, width = upper.shape
     examples = store.shape[0]
     block = pl.BlockSpec((groups, rows, unit), lambda s: (0, 0, s))
+    whole = pl.BlockSpec((2, groups, rows, examples), lambda s: (0, 0, 0, 0))
     return pl.pallas_call(
-        visit_kernel,
+        functools.partial(visit_kernel, len(words)),
         grid=(width // unit,),
         in_specs=[
             block,
             block,
             pl.BlockSpec((examples, unit), lambda s: (0, s + first)),
-            pl.BlockSpec(memory_space=pl.ANY),
-        ],
-        out_specs=pl.BlockSpec((2, groups, rows, examples), lambda s: (0, 0, 0, 0)),
+        ]
+        + [pl.BlockSpec(memory_space=pl.ANY) for _ in words]
+        + [whole for _ in base],
+        out_specs=whole,
         out_shape=jax.ShapeDtypeStruct((2, groups, rows, examples), jnp.float32),
         compiler_params=pltpu.CompilerParams(vmem_limit_bytes=VMEM),
         name="visit",
-    )(upper, lower, store, word)
+    )(upper, lower, store, *words, *base)
 
 
 def shifted(value, axis, steps):
@@ -265,7 +269,7 @@
         pairs = [(i, i ^ 1) for i in range(lax.axis_size("ex"))]
         return lax.ppermute(word, "ex", pairs), came, work
 
-    word, came_raw, mine = both_there(came_raw, mine)
+    word, came_raw, (mine, cuts) = both_there(came_raw, (mine, cuts))
     a, cut, word = together((a, cuts[0], word))
     came_a = send(a)
     came_c = [send(cut)]
@@ -274,19 +278,18 @@
     word, came_a, (scores_raw, own_scores) = both_there(came_a, (scores_raw, own_scores))
     cut, word = together((cuts[1], word))
     came_c.append(send(cut))
-    scores_a = visit(*came_a, store, 0, unit, word)
+    scores_a = visit(*came_a, store, 0, unit, [word])
     both = grp_sum(jnp.concatenate([scores_raw, scores_a], axis=2), 1)
     word, came_c[0], both = both_there(came_c[0], both)
     cut, word = together((cuts[2], word))
     came_c.append(send(cut))
-    part = visit(*came_c[0], store, 0, unit, word)
-    both, came_c[1] = together((both, came_c[1]))
-    upper_scores = [shifted(both[0], "ex", 1)]
-    lower_scores = [shifted(both[1], "ex", -1)]
-    part = part + visit(*came_c[1], store, PIECES[0], unit, word)
-    part = part + visit(*came_c[2], store, PIECES[0] + PIECES[1], unit, word)
-    upper_scores.append(to_owner(part[0], 1))
-    lower_scores.append(to_owner(part[1], -1))
+    part = visit(*came_c[0], store, 0, unit, [word])
+    both, came_c[1], part = together((both, came_c[1], part))
+    returned = shifted(both[0], "ex", 1), shifted(both[1], "ex", -1)
+    part = visit(*came_c[1], store, PIECES[0], unit, [word], part)
+    part = visit(*came_c[2], store, PIECES[0] + PIECES[1], unit, returned, part)
+    upper_scores = [returned[0], to_owner(part[0], 1)]
+    lower_scores = [returned[1], to_owner(part[1], -1)]
 
     scores = jnp.stack(
         [jnp.concatenate(upper_scores), own_scores, jnp.concatenate(lower_scores)]

time: 401 us -> 396 us (0.988)
  waiting for transfers between devices: 241 us -> 236 us
    ppermute x14, waiting for transfers between devices: 238 us -> 231 us  [shifted(): return lax.ppermute(value, axis, pairs)]
  transfers between devices with their start and end apart: 21 -> 21, of which waited for: 8 -> 9; matrix products, arithmetic and copies ran while one was open for 3% -> 3% of each run, Pallas kernels for 30% -> 29%
where the time goes in v3:
time: 396 us; the launch traced here: 394 us
  waiting for transfers between devices  236 us (60%)
  Pallas kernels  119 us (30%)
  starting transfers between devices  21.8 us (6%)
  local copies, waits for them, and re-layouts  11.9 us (3%)
  other arithmetic  4.34 us (1%)
    ppermute x14, waiting for transfers between devices, shifted(): return lax.ppermute(value, axis, pairs)  231 us
    pallas_call x4, Pallas kernels, visit(): pl.pallas_call(functools.partial(visit_kernel, len(words)), grid=(width /...  46.1 us
    pallas_call x1, Pallas kernels, own(): pl.pallas_call(functools.partial(own_kernel, bounds), grid=(modules,), in...  37.7 us
    pallas_call x1, Pallas kernels, visit_raw(): pl.pallas_call(functools.partial(visit_raw_kernel, len(pieces)), grid=(mo...  35.4 us
    ppermute x14, starting transfers between devices, shifted(): return lax.ppermute(value, axis, pairs)  15.6 us
  transfers between devices with their start and end apart: 21, of which 9 were waited for; matrix products, arithmetic and copies ran while one was open for 3% of the time, Pallas kernels for 29%

profile of v3, /device:TPU:1, one launch (start us, length us, event | category | flops | bytes accessed | tf_op | source)
XLA Modules:
  0.0 393.7 jit_solution(4820423941837062484)
XLA Ops:
  0.0 1.7 slice.44
  1.7 0.1 collective-permute-start
  1.8 2.6 collective-permute-start.1
  4.5 37.7 %own.1 = (bf16[2,80,32768]{2,1,0:T(8,128)(2,1)}, bf16[2,32,32768]{2,1,0:T(8,128)(2,1)}, f32[2,128,512]{2,1,0:T(8,128)}) custom-call(bf16[256,32768]{1,0:T(8,128)(2,1)} %x_ref, bf16[8,64,64]{2,1,0:T(8,128)(2,1)} %refs_2_.1, bf16[8,64,64]{2,1,0:T(8,128)(2,1)} %refs_3_.1, bf16[512,32768]{1,0:T(8,128)(2,1)} %slab_ref.9), custom_call_target="tpu_custom_call" | custom-call | tf_op jit(solution)/shard_map/own/pallas_call | solution.py:108
  42.2 3.2 slice.35
  45.4 1.3 slice.36
  46.7 0.8 slice.37
  47.5 3.1 collective-permute-done.refs_0_
  50.7 1.2 collective-permute-done.2.refs_5_
  51.9 0.2 collective-permute-start.5
  52.0 1.6 collective-permute-start.6
  53.6 3.2 collective-permute-start.3
  56.9 1.3 collective-permute-start.7
  58.2 35.4 %visit_raw.1 = f32[2,2,16,512]{3,2,1,0:T(8,128)} custom-call(bf16[2,16,32768]{2,1,0:T(8,128)(2,1)} %copy-done.2, bf16[2,16,32768]{2,1,0:T(8,128)(2,1)} %copy-done.3, bf16[8,64,64]{2,1,0:T(8,128)(2,1)} %refs_2_.1, bf16[8,64,64]{2,1,0:T(8,128)(2,1)} %refs_3_.1, bf16[512,32768]{1,0:T(8,128)(2,1)} %slab_ref.9, bf16[16,128]{1,0:T(8,128)(2,1)} %copy-done.14), custom_call_target="tpu_custom_call" | custom-call | tf_op jit(solution)/shard_map/visit_raw/pallas_call | solution.py:156
  93.6 208.8 %collective-permute-done.5.upper_ref = bf16[2,80,32768]{2,1,0:T(8,128)(2,1)} collective-permute-done((bf16[2,80,32768]{2,1,0:T(8,128)(2,1)}, bf16[2,80,32768]{2,1,0:T(8,128)(2,1)}, u32[]{:S(2)}, u32[]{:S(2)}) %collective-permute-start.5) | collective-permute-done | bytes 10485792 | tf_op jit(solution)/shard_map/ppermute | solution.py:214
  302.3 0.7 slice_bitcast_fusion.2
  303.1 1.2 collective-permute-done.8.rest_0_
  304.3 0.2 collective-permute-start.10
  304.4 1.6 collective-permute-start.11
  306.0 21.8 %visit.4 = f32[2,2,80,512]{3,2,1,0:T(8,128)} custom-call(bf16[2,80,32768]{2,1,0:T(8,128)(2,1)} %collective-permute-done.5.upper_ref, bf16[2,80,32768]{2,1,0:T(8,128)(2,1)} %collective-permute-done.6.lower_ref, bf16[512,32768]{1,0:T(8,128)(2,1)} %slab_ref.9, bf16[80,128]{1,0:T(8,128)(2,1)} %copy-done.13), custom_call_target="tpu_custom_call" | custom-call | tf_op jit(solution)/shard_map/visit/pallas_call | solution.py:194
  327.8 1.0 fusion.1
  328.8 1.3 collective-permute-start.9
  330.1 11.5 %collective-permute-done.3.upper_ref = bf16[2,32,16384]{2,1,0:T(8,128)(2,1)S(1)} collective-permute-done((bf16[2,32,16384]{2,1,0:T(8,128)(2,1)}, bf16[2,32,16384]{2,1,0:T(8,128)(2,1)S(1)}, u32[]{:S(2)}, u32[]{:S(2)}) %collective-permute-start.3) | collective-permute-done | bytes 2097184 | tf_op jit(solution)/shard_map/ppermute | solution.py:214
  341.6 1.3 fusion.4
  343.0 1.2 collective-permute-done.12.rest_0_
  344.1 0.2 collective-permute-start.14
  344.3 1.6 collective-permute-start.15
  345.9 10.6 %visit.5.rest_1_ = f32[2,2,32,512]{3,2,1,0:T(8,128)} custom-call(bf16[2,32,16384]{2,1,0:T(8,128)(2,1)} %copy-done.1, bf16[2,32,16384]{2,1,0:T(8,128)(2,1)} %collective-permute-done.4.lower_ref, bf16[512,32768]{1,0:T(8,128)(2,1)} %slab_ref.9, bf16[32,128]{1,0:T(8,128)(2,1)} %copy-done.12), custom_call_target="tpu_custom_call" | custom-call | tf_op jit(solution)/shard_map/visit/pallas_call | solution.py:194
  356.5 7.6 %collective-permute-done.10.upper_ref = bf16[2,32,12288]{2,1,0:T(8,128)(2,1)} collective-permute-done((bf16[2,32,12288]{2,1,0:T(8,128)(2,1)S(1)}, bf16[2,32,12288]{2,1,0:T(8,128)(2,1)}, u32[]{:S(2)}, u32[]{:S(2)}) %collective-permute-start.10) | collective-permute-done | bytes 1572896 | tf_op jit(solution)/shard_map/ppermute | solution.py:214
  364.1 0.8 slice_bitcast_fusion
  364.9 1.8 collective-permute-start.13
  366.8 0.1 broadcast_in_dim.6
  366.9 0.1 reshape.21
  367.0 0.3 copy.7
  367.3 9.0 %visit.6.rest_2_ = f32[2,2,32,512]{3,2,1,0:T(8,128)} custom-call(bf16[2,32,12288]{2,1,0:T(8,128)(2,1)} %collective-permute-done.10.upper_ref, bf16[2,32,12288]{2,1,0:T(8,128)(2,1)} %collective-permute-done.11.lower_ref, bf16[512,32768]{1,0:T(8,128)(2,1)} %slab_ref.9, bf16[32,128]{1,0:T(8,128)(2,1)} %copy-done.12, f32[2,2,32,512]{3,2,1,0:T(8,128)} %visit.5.rest_1_), custom_call_target="tpu_custom_call" | custom-call | tf_op jit(solution)/shard_map/visit/pallas_call | solution.py:194
  376.4 0.7 copy-done.9
  377.1 0.2 copy-done.10
  377.4 0.7 copy-done.6
  378.0 4.7 %visit.7 = f32[2,2,32,512]{3,2,1,0:T(8,128)} custom-call(bf16[2,32,4096]{2,1,0:T(8,128)(2,1)} %copy-done.9, bf16[2,32,4096]{2,1,0:T(8,128)(2,1)} %copy-done.10, bf16[512,32768]{1,0:T(8,128)(2,1)} %slab_ref.9, f32[96,512]{1,0:T(8,128)} %copy-done.8, f32[96,512]{1,0:T(8,128)} %copy-done.6, f32[2,2,32,512]{3,2,1,0:T(8,128)} %visit.6.rest_2_), custom_call_target="tpu_custom_call" | custom-call | tf_op jit(solution)/shard_map/visit/pallas_call | solution.py:194
  382.8 1.0 fusion.5
  383.8 1.8 collective-permute-start.17
  385.6 1.0 collective-permute-start.18
  386.6 0.7 collective-permute-start.19
  387.3 2.7 collective-permute-start.20
  390.0 0.9 maximum_bitcast_fusion
  390.9 0.4 collective-permute-done.19
  391.3 1.3 collective-permute-done.20
  392.6 1.0 maximum_multiply_fusion
  (59 shorter events, 0.6 us)
Async XLA Ops:
  1.7 48.9 %collective-permute-start = (bf16[2,16,32768]{2,1,0:T(8,128)(2,1)S(1)}, bf16[2,16,32768]{2,1,0:T(8,128)(2,1)S(1)}, u32[]{:S(2)}, u32[]{:S(2)}) collective-permute-start(bf16[2,16,32768]{2,1,0:T(8,128)(2,1)S(1)} %slice.44), channel_id=1, source_target_pairs={{0,30},{2,0},{4,2},{6,4},{8,6},{10,8},{12,10},{14,12},{16,14},{18,... | collective-permute-start | bytes 6291464 | tf_op jit(solution)/shard_map/ppermute | solution.py:214
  1.8 48.8 %collective-permute-start.1 = (bf16[2,16,32768]{2,1,0:T(8,128)(2,1)S(1)}, bf16[2,16,32768]{2,1,0:T(8,128)(2,1)S(1)}, u32[]{:S(2)}, u32[]{:S(2)}) collective-permute-start(bf16[2,16,32768]{2,1,0:T(8,128)(2,1)S(1)} %slice.44), channel_id=1, source_target_pairs={{0,2},{2,4},{4,6},{6,8},{8,10},{10,12},{12,14},{14,16},{16,18},{18... | collective-permute-start | bytes 6291464 | tf_op jit(solution)/shard_map/ppermute | solution.py:214
  42.2 3.2 copy-start
  45.4 11.4 %copy-start.11 = (f32[2,128,512]{2,1,0:T(8,128)S(1)}, f32[2,128,512]{2,1,0:T(8,128)}, u32[]{:S(2)}) copy-start(f32[2,128,512]{2,1,0:T(8,128)} %get-tuple-element.49) | copy-start | bytes 1572868
  50.6 1.4 copy-start.2
  50.6 3.0 copy-start.3
  50.6 1.2 collective-permute-start.2
  51.9 6.3 %copy-start.14 = (bf16[16,128]{1,0:T(8,128)(2,1)}, bf16[16,128]{1,0:T(8,128)(2,1)S(1)}, u32[]{:S(2)}) copy-start(bf16[16,128]{1,0:T(8,128)(2,1)S(1)} %collective-permute-done.2.refs_5_) | copy-start | bytes 12292
  51.9 250.5 %collective-permute-start.5 = (bf16[2,80,32768]{2,1,0:T(8,128)(2,1)}, bf16[2,80,32768]{2,1,0:T(8,128)(2,1)}, u32[]{:S(2)}, u32[]{:S(2)}) collective-permute-start(bf16[2,80,32768]{2,1,0:T(8,128)(2,1)} %get-tuple-element.45), channel_id=1, source_target_pairs={{0,30},{2,0},{4,2},{6,4},{8,6},{10,8},{12,10},{14,12},{16,14},{18,... | collective-permute-start | bytes 31457288 | tf_op jit(solution)/shard_map/ppermute | solution.py:214
  52.0 251.0 %collective-permute-start.6 = (bf16[2,80,32768]{2,1,0:T(8,128)(2,1)}, bf16[2,80,32768]{2,1,0:T(8,128)(2,1)}, u32[]{:S(2)}, u32[]{:S(2)}) collective-permute-start(bf16[2,80,32768]{2,1,0:T(8,128)(2,1)} %get-tuple-element.45), channel_id=1, source_target_pairs={{0,2},{2,4},{4,6},{6,8},{8,10},{10,12},{12,14},{14,16},{16,18},{18... | collective-permute-start | bytes 31457288 | tf_op jit(solution)/shard_map/ppermute | solution.py:214
  53.6 287.9 %collective-permute-start.3 = (bf16[2,32,16384]{2,1,0:T(8,128)(2,1)}, bf16[2,32,16384]{2,1,0:T(8,128)(2,1)S(1)}, u32[]{:S(2)}, u32[]{:S(2)}) collective-permute-start(bf16[2,32,16384]{2,1,0:T(8,128)(2,1)} %slice.35), channel_id=1, source_target_pairs={{0,30},{2,0},{4,2},{6,4},{8,6},{10,8},{12,10},{14,12},{16,14},{18,... | collective-permute-start | bytes 6291464 | tf_op jit(solution)/shard_map/ppermute | solution.py:214
  56.9 36.7 %collective-permute-start.7 = (f32[128,512]{1,0:T(8,128)S(1)}, f32[128,512]{1,0:T(8,128)S(1)}, u32[]{:S(2)}, u32[]{:S(2)}) collective-permute-start(f32[128,512]{1,0:T(8,128)S(1)} %dynamic-slice_bitcast_fusion), channel_id=1, source_target_pairs={{0,1},{1,0},{2,3},{3,2},{4,5},{5,4},{6,7},{7,6},{8,9},{9,8},{10,11... | collective-permute-start | bytes 786440 | tf_op jit(solution)/shard_map/ppermute | solution.py:214
  58.1 284.7 %collective-permute-start.4 = (bf16[2,32,16384]{2,1,0:T(8,128)(2,1)}, bf16[2,32,16384]{2,1,0:T(8,128)(2,1)}, u32[]{:S(2)}, u32[]{:S(2)}) collective-permute-start(bf16[2,32,16384]{2,1,0:T(8,128)(2,1)} %slice.35), channel_id=1, source_target_pairs={{0,2},{2,4},{4,6},{6,8},{8,10},{10,12},{12,14},{14,16},{16,18},{18... | collective-permute-start | bytes 6291464 | tf_op jit(solution)/shard_map/ppermute | solution.py:214
  58.2 246.1 %copy-start.4 = (bf16[2,32,12288]{2,1,0:T(8,128)(2,1)S(1)}, bf16[2,32,12288]{2,1,0:T(8,128)(2,1)}, u32[]{:S(2)}) copy-start(bf16[2,32,12288]{2,1,0:T(8,128)(2,1)} %slice.36) | copy-start | bytes 4718596
  303.1 24.7 %copy-start.5 = (f32[2,2,16,512]{3,2,1,0:T(8,128)S(1)}, f32[2,2,16,512]{3,2,1,0:T(8,128)}, u32[]{:S(2)}) copy-start(f32[2,2,16,512]{3,2,1,0:T(8,128)} %visit_raw.1) | copy-start | bytes 393220
  303.1 1.2 collective-permute-start.8
  304.3 1.8 copy-start.13
  304.3 59.9 %collective-permute-start.10 = (bf16[2,32,12288]{2,1,0:T(8,128)(2,1)S(1)}, bf16[2,32,12288]{2,1,0:T(8,128)(2,1)}, u32[]{:S(2)}, u32[]{:S(2)}) collective-permute-start(bf16[2,32,12288]{2,1,0:T(8,128)(2,1)S(1)} %copy-done.4), channel_id=1, source_target_pairs={{0,30},{2,0},{4,2},{6,4},{8,6},{10,8},{12,10},{14,12},{16,14},{18,... | collective-permute-start | bytes 4718600 | tf_op jit(solution)/shard_map/ppermute | solution.py:214
  304.4 59.7 %collective-permute-start.11 = (bf16[2,32,12288]{2,1,0:T(8,128)(2,1)S(1)}, bf16[2,32,12288]{2,1,0:T(8,128)(2,1)}, u32[]{:S(2)}, u32[]{:S(2)}) collective-permute-start(bf16[2,32,12288]{2,1,0:T(8,128)(2,1)S(1)} %copy-done.4), channel_id=1, source_target_pairs={{0,2},{2,4},{4,6},{6,8},{8,10},{10,12},{12,14},{14,16},{16,18},{18... | collective-permute-start | bytes 4718600 | tf_op jit(solution)/shard_map/ppermute | solution.py:214
  328.8 12.8 %collective-permute-start.9 = (f32[2,96,512]{2,1,0:T(8,128)S(1)}, f32[2,96,512]{2,1,0:T(8,128)S(1)}, u32[]{:S(2)}, u32[]{:S(2)}) collective-permute-start(f32[2,96,512]{2,1,0:T(8,128)S(1)} %fusion.1), channel_id=1, source_target_pairs={{0,1},{1,0},{2,3},{3,2},{4,5},{5,4},{6,7},{7,6},{8,9},{9,8},{10,11... | collective-permute-start | bytes 1179656 | tf_op jit(solution)/shard_map/ppermute | solution.py:214
  341.6 4.3 %copy-start.1 = (bf16[2,32,16384]{2,1,0:T(8,128)(2,1)}, bf16[2,32,16384]{2,1,0:T(8,128)(2,1)S(1)}, u32[]{:S(2)}) copy-start(bf16[2,32,16384]{2,1,0:T(8,128)(2,1)S(1)} %collective-permute-done.3.upper_ref) | copy-start | bytes 6291460
  342.9 23.8 %copy-start.15 = (s32[8,24]{1,0:T(8,128)S(1)}, s32[8,24]{1,0:T(8,128)}, u32[]{:S(2)}) copy-start(s32[8,24]{1,0:T(8,128)} %param.9) | copy-start | bytes 2308
  342.9 1.2 collective-permute-start.12
  344.1 1.8 copy-start.12
  344.1 32.2 %collective-permute-start.14 = (bf16[2,32,4096]{2,1,0:T(8,128)(2,1)}, bf16[2,32,4096]{2,1,0:T(8,128)(2,1)S(1)}, u32[]{:S(2)}, u32[]{:S(2)}) collective-permute-start(bf16[2,32,4096]{2,1,0:T(8,128)(2,1)} %slice.37), channel_id=1, source_target_pairs={{0,30},{2,0},{4,2},{6,4},{8,6},{10,8},{12,10},{14,12},{16,14},{18,... | collective-permute-start | bytes 1572872 | tf_op jit(solution)/shard_map/ppermute | solution.py:214
  344.3 32.0 %collective-permute-start.15 = (bf16[2,32,4096]{2,1,0:T(8,128)(2,1)}, bf16[2,32,4096]{2,1,0:T(8,128)(2,1)S(1)}, u32[]{:S(2)}, u32[]{:S(2)}) collective-permute-start(bf16[2,32,4096]{2,1,0:T(8,128)(2,1)} %slice.37), channel_id=1, source_target_pairs={{0,2},{2,4},{4,6},{6,8},{8,10},{10,12},{12,14},{14,16},{16,18},{18... | collective-permute-start | bytes 1572872 | tf_op jit(solution)/shard_map/ppermute | solution.py:214
  364.9 11.4 %collective-permute-start.13 = (f32[96,512]{1,0:T(8,128)}, f32[96,512]{1,0:T(8,128)S(1)}, u32[]{:S(2)}, u32[]{:S(2)}) collective-permute-start(f32[96,512]{1,0:T(8,128)} %get-tuple-element.70), channel_id=1, source_target_pairs={{0,2},{2,4},{4,6},{6,8},{8,10},{10,12},{12,14},{14,16},{16,18},{18... | collective-permute-start | bytes 589832 | tf_op jit(solution)/shard_map/ppermute | solution.py:214
  366.7 9.7 %collective-permute-start.16 = (f32[96,512]{1,0:T(8,128)}, f32[96,512]{1,0:T(8,128)S(1)}, u32[]{:S(2)}, u32[]{:S(2)}) collective-permute-start(f32[96,512]{1,0:T(8,128)} %get-tuple-element.69), channel_id=1, source_target_pairs={{0,30},{2,0},{4,2},{6,4},{8,6},{10,8},{12,10},{14,12},{16,14},{18,... | collective-permute-start | bytes 589832 | tf_op jit(solution)/shard_map/ppermute | solution.py:214
  376.3 0.8 copy-start.9
  376.3 0.9 copy-start.10
  376.4 1.0 copy-start.8
  377.4 0.7 copy-start.6
  382.8 9.8 %copy-start.7 = (f32[96,512]{1,0:T(8,128)S(1)}, f32[96,512]{1,0:T(8,128)}, u32[]{:S(2)}) copy-start(f32[96,512]{1,0:T(8,128)} %copy-done.6) | copy-start | bytes 589828
  383.8 6.1 %collective-permute-start.17 = (f32[32,512]{1,0:T(8,128)S(1)}, f32[32,512]{1,0:T(8,128)S(1)}, u32[]{:S(2)}, u32[]{:S(2)}) collective-permute-start(f32[32,512]{1,0:T(8,128)S(1)} %get-tuple-element.74), channel_id=1, source_target_pairs={{0,2},{1,3},{2,4},{3,5},{4,6},{5,7},{6,8},{7,9},{8,10},{9,11},{10,... | collective-permute-start | bytes 196616 | tf_op jit(solution)/shard_map/ppermute | solution.py:239
  385.6 4.3 %collective-permute-start.18 = (f32[32,512]{1,0:T(8,128)S(1)}, f32[32,512]{1,0:T(8,128)S(1)}, u32[]{:S(2)}, u32[]{:S(2)}) collective-permute-start(f32[32,512]{1,0:T(8,128)S(1)} %get-tuple-element.73), channel_id=1, source_target_pairs={{0,3},{1,2},{2,5},{3,4},{4,7},{5,6},{6,9},{7,8},{8,11},{9,10},{10,... | collective-permute-start | bytes 196616 | tf_op jit(solution)/shard_map/ppermute | solution.py:239
  386.6 4.7 %collective-permute-start.19 = (f32[32,512]{1,0:T(8,128)S(1)}, f32[32,512]{1,0:T(8,128)S(1)}, u32[]{:S(2)}, u32[]{:S(2)}) collective-permute-start(f32[32,512]{1,0:T(8,128)S(1)} %get-tuple-element.76), channel_id=1, source_target_pairs={{0,30},{1,31},{2,0},{3,1},{4,2},{5,3},{6,4},{7,5},{8,6},{9,7},{10,... | collective-permute-start | bytes 196616 | tf_op jit(solution)/shard_map/ppermute | solution.py:239
  387.3 5.3 %collective-permute-start.20 = (f32[32,512]{1,0:T(8,128)S(1)}, f32[32,512]{1,0:T(8,128)S(1)}, u32[]{:S(2)}, u32[]{:S(2)}) collective-permute-start(f32[32,512]{1,0:T(8,128)S(1)} %get-tuple-element.75), channel_id=1, source_target_pairs={{0,31},{1,30},{2,1},{3,0},{4,3},{5,2},{6,5},{7,4},{8,7},{9,6},{10,... | collective-permute-start | bytes 196616 | tf_op jit(solution)/shard_map/ppermute | solution.py:239

commit v4 on v3

--- a/solution.py
+++ b/solution.py
@@ -9,8 +9,8 @@
 
 QB = 32
 SUB = 64
-CHUNKS = (2, 10, 4)
-PIECES = (4, 3, 1)
+CHUNKS = (2, 8, 6)
+PIECES = (5, 2, 1)
 WIDE = 256
 LOW = 8
 LANES = 128

time: 396 us -> 395 us (level)
  waiting for transfers between devices: 236 us -> 232 us
    ppermute x14, waiting for transfers between devices: 231 us -> 226 us  [shifted(): return lax.ppermute(value, axis, pairs)]
  transfers between devices with their start and end apart: 21 -> 21, of which waited for: 9 -> 10; matrix products, arithmetic and copies ran while one was open for 3% -> 4% of each run, Pallas kernels for 29% -> 29%
where the time goes in v4:
time: 395 us; the launch traced here: 394 us
  waiting for transfers between devices  232 us (59%)
  Pallas kernels  118 us (30%)
  starting transfers between devices  23.8 us (6%)
  local copies, waits for them, and re-layouts  14.7 us (4%)
  other arithmetic  4.93 us (1%)
    ppermute x14, waiting for transfers between devices, shifted(): return lax.ppermute(value, axis, pairs)  226 us
    pallas_call x4, Pallas kernels, visit(): pl.pallas_call(functools.partial(visit_kernel, len(words)), grid=(width /...  45.3 us
    pallas_call x1, Pallas kernels, own(): pl.pallas_call(functools.partial(own_kernel, bounds), grid=(modules,), in...  37.7 us
    pallas_call x1, Pallas kernels, visit_raw(): pl.pallas_call(functools.partial(visit_raw_kernel, len(pieces)), grid=(mo...  35.4 us
    ppermute x14, starting transfers between devices, shifted(): return lax.ppermute(value, axis, pairs)  14.7 us
    slice x3, local copies, waits for them, and re-layouts, body(): cuts.append(c[..., start * unit:(start + count) * unit])  9.04 us
  transfers between devices with their start and end apart: 21, of which 10 were waited for; matrix products, arithmetic and copies ran while one was open for 4% of the time, Pallas kernels for 29%

profile of v4, /device:TPU:1, one launch (start us, length us, event | category | flops | bytes accessed | tf_op | source)
XLA Modules:
  0.0 393.6 jit_solution(11264214043313292821)
XLA Ops:
  0.0 1.7 slice.44
  1.7 0.1 collective-permute-start
  1.8 2.6 collective-permute-start.1
  4.5 37.7 %own.1 = (bf16[2,64,32768]{2,1,0:T(8,128)(2,1)}, bf16[2,48,32768]{2,1,0:T(8,128)(2,1)}, f32[2,128,512]{2,1,0:T(8,128)}) custom-call(bf16[256,32768]{1,0:T(8,128)(2,1)} %x_ref, bf16[8,64,64]{2,1,0:T(8,128)(2,1)} %refs_2_.1, bf16[8,64,64]{2,1,0:T(8,128)(2,1)} %refs_3_.1, bf16[512,32768]{1,0:T(8,128)(2,1)} %slab_ref.9), custom_call_target="tpu_custom_call" | custom-call | tf_op jit(solution)/shard_map/own/pallas_call | solution.py:108
  42.2 4.3 %slice.35 = bf16[2,48,20480]{2,1,0:T(8,128)(2,1)} slice(bf16[2,48,32768]{2,1,0:T(8,128)(2,1)} %get-tuple-element.41), slice={[0:2], [0:48], [0:20480]} | slice | bytes 7864320 | tf_op jit(solution)/shard_map/slice | solution.py:264
  46.5 2.7 slice.36
  49.2 2.1 slice.37
  51.3 2.9 collective-permute-start.2
  54.1 0.8 collective-permute-done.2.refs_5_
  55.0 0.3 collective-permute-start.5
  55.3 1.4 collective-permute-start.6
  56.7 3.0 collective-permute-start.3
  59.8 1.3 collective-permute-start.7
  61.0 35.4 %visit_raw.1 = f32[2,2,16,512]{3,2,1,0:T(8,128)} custom-call(bf16[2,16,32768]{2,1,0:T(8,128)(2,1)} %copy-done, bf16[2,16,32768]{2,1,0:T(8,128)(2,1)} %collective-permute-done.1.refs_1_, bf16[8,64,64]{2,1,0:T(8,128)(2,1)} %refs_2_.1, bf16[8,64,64]{2,1,0:T(8,128)(2,1)} %refs_3_.1, bf16[512,32768]{1,0:T(8,128)(2,1)} %slab_ref.9, bf16[16,128]{1,0:T(8,128)(2,1)} %copy-done.7), custom_call_target="tpu_custom_call" | custom-call | tf_op jit(solution)/shard_map/visit_raw/pallas_call | solution.py:156
  96.5 183.6 %collective-permute-done.5.upper_ref = bf16[2,64,32768]{2,1,0:T(8,128)(2,1)} collective-permute-done((bf16[2,64,32768]{2,1,0:T(8,128)(2,1)}, bf16[2,64,32768]{2,1,0:T(8,128)(2,1)}, u32[]{:S(2)}, u32[]{:S(2)}) %collective-permute-start.5) | collective-permute-done | bytes 8388640 | tf_op jit(solution)/shard_map/ppermute | solution.py:214
  280.2 0.7 slice_bitcast_fusion.2
  280.9 1.2 collective-permute-done.8.rest_0_
  282.1 0.2 collective-permute-start.10
  282.2 1.6 collective-permute-start.11
  283.8 19.9 %visit.4 = f32[2,2,64,512]{3,2,1,0:T(8,128)} custom-call(bf16[2,64,32768]{2,1,0:T(8,128)(2,1)} %collective-permute-done.5.upper_ref, bf16[2,64,32768]{2,1,0:T(8,128)(2,1)} %collective-permute-done.6.lower_ref, bf16[512,32768]{1,0:T(8,128)(2,1)} %slab_ref.9, bf16[64,128]{1,0:T(8,128)(2,1)} %copy-done.6), custom_call_target="tpu_custom_call" | custom-call | tf_op jit(solution)/shard_map/visit/pallas_call | solution.py:194
  303.7 1.0 fusion.1
  304.7 1.3 collective-permute-start.9
  306.0 33.2 %collective-permute-done.3.upper_ref = bf16[2,48,20480]{2,1,0:T(8,128)(2,1)} collective-permute-done((bf16[2,48,20480]{2,1,0:T(8,128)(2,1)}, bf16[2,48,20480]{2,1,0:T(8,128)(2,1)}, u32[]{:S(2)}, u32[]{:S(2)}) %collective-permute-start.3) | collective-permute-done | bytes 3932192 | tf_op jit(solution)/shard_map/ppermute | solution.py:214
  339.1 0.7 slice_bitcast_fusion.3
  339.9 1.0 fusion.4
  341.0 1.2 collective-permute-done.12.rest_0_
  342.1 0.2 collective-permute-start.14
  342.3 1.6 collective-permute-start.15
  343.9 13.6 %visit.5.rest_1_ = f32[2,2,48,512]{3,2,1,0:T(8,128)} custom-call(bf16[2,48,20480]{2,1,0:T(8,128)(2,1)} %collective-permute-done.3.upper_ref, bf16[2,48,20480]{2,1,0:T(8,128)(2,1)} %collective-permute-done.4.lower_ref, bf16[512,32768]{1,0:T(8,128)(2,1)} %slab_ref.9, bf16[48,128]{1,0:T(8,128)(2,1)} %copy-done.5), custom_call_target="tpu_custom_call" | custom-call | tf_op jit(solution)/shard_map/visit/pallas_call | solution.py:194
  357.5 6.9 %collective-permute-done.10.upper_ref = bf16[2,48,8192]{2,1,0:T(8,128)(2,1)S(1)} collective-permute-done((bf16[2,48,8192]{2,1,0:T(8,128)(2,1)S(1)}, bf16[2,48,8192]{2,1,0:T(8,128)(2,1)S(1)}, u32[]{:S(2)}, u32[]{:S(2)}) %collective-permute-start.10) | collective-permute-done | bytes 1572896 | tf_op jit(solution)/shard_map/ppermute | solution.py:214
  364.3 0.8 slice_bitcast_fusion
  365.1 1.1 collective-permute-start.13
  366.4 0.1 reshape.21
  366.5 0.3 copy.7
  366.8 6.9 %visit.6.rest_2_ = f32[2,2,48,512]{3,2,1,0:T(8,128)} custom-call(bf16[2,48,8192]{2,1,0:T(8,128)(2,1)} %copy-done.1, bf16[2,48,8192]{2,1,0:T(8,128)(2,1)} %collective-permute-done.11.lower_ref, bf16[512,32768]{1,0:T(8,128)(2,1)} %slab_ref.9, bf16[48,128]{1,0:T(8,128)(2,1)} %copy-done.5, f32[2,2,48,512]{3,2,1,0:T(8,128)} %visit.5.rest_1_), custom_call_target="tpu_custom_call" | custom-call | tf_op jit(solution)/shard_map/visit/pallas_call | solution.py:194
  373.7 0.9 collective-permute-done.14.upper_ref
  374.6 0.3 collective-permute-done.13.rest_0_
  374.9 1.5 collective-permute-done.16.rest_1_
  376.4 5.0 %visit.7 = f32[2,2,48,512]{3,2,1,0:T(8,128)} custom-call(bf16[2,48,4096]{2,1,0:T(8,128)(2,1)} %collective-permute-done.14.upper_ref, bf16[2,48,4096]{2,1,0:T(8,128)(2,1)} %collective-permute-done.15.lower_ref, bf16[512,32768]{1,0:T(8,128)(2,1)} %slab_ref.9, f32[80,512]{1,0:T(8,128)} %collective-permute-done.13.rest_0_, ...), custom_call_target="tpu_custom_call" | custom-call | tf_op jit(solution)/shard_map/visit/pallas_call | solution.py:194
  381.3 1.0 fusion.5
  382.4 1.1 collective-permute-start.17
  383.5 1.0 collective-permute-start.18
  384.5 0.7 collective-permute-start.19
  385.2 3.4 collective-permute-start.20
  388.6 0.9 maximum_bitcast_fusion
  389.5 2.1 collective-permute-done.20
  391.6 0.9 maximum_bitcast_fusion.1
  392.6 1.0 maximum_multiply_fusion
  (45 shorter events, 0.5 us)
Async XLA Ops:
  1.7 49.5 %collective-permute-start = (bf16[2,16,32768]{2,1,0:T(8,128)(2,1)S(1)}, bf16[2,16,32768]{2,1,0:T(8,128)(2,1)S(1)}, u32[]{:S(2)}, u32[]{:S(2)}) collective-permute-start(bf16[2,16,32768]{2,1,0:T(8,128)(2,1)S(1)} %slice.44), channel_id=1, source_target_pairs={{0,30},{2,0},{4,2},{6,4},{8,6},{10,8},{12,10},{14,12},{16,14},{18,... | collective-permute-start | bytes 6291464 | tf_op jit(solution)/shard_map/ppermute | solution.py:214
  1.8 49.4 %collective-permute-start.1 = (bf16[2,16,32768]{2,1,0:T(8,128)(2,1)S(1)}, bf16[2,16,32768]{2,1,0:T(8,128)(2,1)}, u32[]{:S(2)}, u32[]{:S(2)}) collective-permute-start(bf16[2,16,32768]{2,1,0:T(8,128)(2,1)S(1)} %slice.44), channel_id=1, source_target_pairs={{0,2},{2,4},{4,6},{6,8},{8,10},{10,12},{12,14},{14,16},{16,18},{18... | collective-permute-start | bytes 6291464 | tf_op jit(solution)/shard_map/ppermute | solution.py:214
  46.4 13.3 %copy-start.4 = (f32[2,128,512]{2,1,0:T(8,128)S(1)}, f32[2,128,512]{2,1,0:T(8,128)}, u32[]{:S(2)}) copy-start(f32[2,128,512]{2,1,0:T(8,128)} %get-tuple-element.49) | copy-start | bytes 1572868
  51.2 9.8 %copy-start = (bf16[2,16,32768]{2,1,0:T(8,128)(2,1)}, bf16[2,16,32768]{2,1,0:T(8,128)(2,1)S(1)}, u32[]{:S(2)}) copy-start(bf16[2,16,32768]{2,1,0:T(8,128)(2,1)S(1)} %collective-permute-done.refs_0_) | copy-start | bytes 6291460
  51.3 3.7 collective-permute-start.2
  55.0 6.1 %copy-start.7 = (bf16[16,128]{1,0:T(8,128)(2,1)}, bf16[16,128]{1,0:T(8,128)(2,1)S(1)}, u32[]{:S(2)}) copy-start(bf16[16,128]{1,0:T(8,128)(2,1)S(1)} %collective-permute-done.2.refs_5_) | copy-start | bytes 12292
  55.0 225.2 %collective-permute-start.5 = (bf16[2,64,32768]{2,1,0:T(8,128)(2,1)}, bf16[2,64,32768]{2,1,0:T(8,128)(2,1)}, u32[]{:S(2)}, u32[]{:S(2)}) collective-permute-start(bf16[2,64,32768]{2,1,0:T(8,128)(2,1)} %get-tuple-element.45), channel_id=1, source_target_pairs={{0,30},{2,0},{4,2},{6,4},{8,6},{10,8},{12,10},{14,12},{16,14},{18,... | collective-permute-start | bytes 25165832 | tf_op jit(solution)/shard_map/ppermute | solution.py:214
  55.3 225.6 %collective-permute-start.6 = (bf16[2,64,32768]{2,1,0:T(8,128)(2,1)}, bf16[2,64,32768]{2,1,0:T(8,128)(2,1)}, u32[]{:S(2)}, u32[]{:S(2)}) collective-permute-start(bf16[2,64,32768]{2,1,0:T(8,128)(2,1)} %get-tuple-element.45), channel_id=1, source_target_pairs={{0,2},{2,4},{4,6},{6,8},{8,10},{10,12},{12,14},{14,16},{16,18},{18... | collective-permute-start | bytes 25165832 | tf_op jit(solution)/shard_map/ppermute | solution.py:214
  56.7 282.4 %collective-permute-start.3 = (bf16[2,48,20480]{2,1,0:T(8,128)(2,1)}, bf16[2,48,20480]{2,1,0:T(8,128)(2,1)}, u32[]{:S(2)}, u32[]{:S(2)}) collective-permute-start(bf16[2,48,20480]{2,1,0:T(8,128)(2,1)} %slice.35), channel_id=1, source_target_pairs={{0,30},{2,0},{4,2},{6,4},{8,6},{10,8},{12,10},{14,12},{16,14},{18,... | collective-permute-start | bytes 11796488 | tf_op jit(solution)/shard_map/ppermute | solution.py:214
  59.7 281.1 %collective-permute-start.4 = (bf16[2,48,20480]{2,1,0:T(8,128)(2,1)}, bf16[2,48,20480]{2,1,0:T(8,128)(2,1)}, u32[]{:S(2)}, u32[]{:S(2)}) collective-permute-start(bf16[2,48,20480]{2,1,0:T(8,128)(2,1)} %slice.35), channel_id=1, source_target_pairs={{0,2},{2,4},{4,6},{6,8},{8,10},{10,12},{12,14},{14,16},{16,18},{18... | collective-permute-start | bytes 11796488 | tf_op jit(solution)/shard_map/ppermute | solution.py:214
  59.8 36.7 %collective-permute-start.7 = (f32[128,512]{1,0:T(8,128)S(1)}, f32[128,512]{1,0:T(8,128)S(1)}, u32[]{:S(2)}, u32[]{:S(2)}) collective-permute-start(f32[128,512]{1,0:T(8,128)S(1)} %dynamic-slice_bitcast_fusion), channel_id=1, source_target_pairs={{0,1},{1,0},{2,3},{3,2},{4,5},{5,4},{6,7},{7,6},{8,9},{9,8},{10,11... | collective-permute-start | bytes 786440 | tf_op jit(solution)/shard_map/ppermute | solution.py:214
  61.0 221.0 %copy-start.2 = (bf16[2,48,8192]{2,1,0:T(8,128)(2,1)S(1)}, bf16[2,48,8192]{2,1,0:T(8,128)(2,1)}, u32[]{:S(2)}) copy-start(bf16[2,48,8192]{2,1,0:T(8,128)(2,1)} %slice.36) | copy-start | bytes 4718596
  280.9 22.8 %copy-start.3 = (f32[2,2,16,512]{3,2,1,0:T(8,128)S(1)}, f32[2,2,16,512]{3,2,1,0:T(8,128)}, u32[]{:S(2)}) copy-start(f32[2,2,16,512]{3,2,1,0:T(8,128)} %visit_raw.1) | copy-start | bytes 393220
  280.9 1.2 collective-permute-start.8
  282.1 1.8 copy-start.6
  282.1 82.2 %collective-permute-start.10 = (bf16[2,48,8192]{2,1,0:T(8,128)(2,1)S(1)}, bf16[2,48,8192]{2,1,0:T(8,128)(2,1)S(1)}, u32[]{:S(2)}, u32[]{:S(2)}) collective-permute-start(bf16[2,48,8192]{2,1,0:T(8,128)(2,1)S(1)} %copy-done.2), channel_id=1, source_target_pairs={{0,30},{2,0},{4,2},{6,4},{8,6},{10,8},{12,10},{14,12},{16,14},{18,... | collective-permute-start | bytes 4718600 | tf_op jit(solution)/shard_map/ppermute | solution.py:214
  282.2 82.1 %collective-permute-start.11 = (bf16[2,48,8192]{2,1,0:T(8,128)(2,1)S(1)}, bf16[2,48,8192]{2,1,0:T(8,128)(2,1)}, u32[]{:S(2)}, u32[]{:S(2)}) collective-permute-start(bf16[2,48,8192]{2,1,0:T(8,128)(2,1)S(1)} %copy-done.2), channel_id=1, source_target_pairs={{0,2},{2,4},{4,6},{6,8},{8,10},{10,12},{12,14},{14,16},{16,18},{18... | collective-permute-start | bytes 4718600 | tf_op jit(solution)/shard_map/ppermute | solution.py:214
  304.7 35.2 %collective-permute-start.9 = (f32[2,80,512]{2,1,0:T(8,128)S(1)}, f32[2,80,512]{2,1,0:T(8,128)S(1)}, u32[]{:S(2)}, u32[]{:S(2)}) collective-permute-start(f32[2,80,512]{2,1,0:T(8,128)S(1)} %fusion.1), channel_id=1, source_target_pairs={{0,1},{1,0},{2,3},{3,2},{4,5},{5,4},{6,7},{7,6},{8,9},{9,8},{10,11... | collective-permute-start | bytes 983048 | tf_op jit(solution)/shard_map/ppermute | solution.py:214
  340.9 25.3 %copy-start.8 = (s32[8,24]{1,0:T(8,128)S(1)}, s32[8,24]{1,0:T(8,128)}, u32[]{:S(2)}) copy-start(s32[8,24]{1,0:T(8,128)} %param.9) | copy-start | bytes 2308
  340.9 1.2 collective-permute-start.12
  342.1 1.8 copy-start.5
  342.1 32.5 %collective-permute-start.14 = (bf16[2,48,4096]{2,1,0:T(8,128)(2,1)}, bf16[2,48,4096]{2,1,0:T(8,128)(2,1)}, u32[]{:S(2)}, u32[]{:S(2)}) collective-permute-start(bf16[2,48,4096]{2,1,0:T(8,128)(2,1)} %slice.37), channel_id=1, source_target_pairs={{0,30},{2,0},{4,2},{6,4},{8,6},{10,8},{12,10},{14,12},{16,14},{18,... | collective-permute-start | bytes 2359304 | tf_op jit(solution)/shard_map/ppermute | solution.py:214
  342.3 32.3 %collective-permute-start.15 = (bf16[2,48,4096]{2,1,0:T(8,128)(2,1)}, bf16[2,48,4096]{2,1,0:T(8,128)(2,1)}, u32[]{:S(2)}, u32[]{:S(2)}) collective-permute-start(bf16[2,48,4096]{2,1,0:T(8,128)(2,1)} %slice.37), channel_id=1, source_target_pairs={{0,2},{2,4},{4,6},{6,8},{8,10},{10,12},{12,14},{14,16},{16,18},{18... | collective-permute-start | bytes 2359304 | tf_op jit(solution)/shard_map/ppermute | solution.py:214
  364.3 2.5 copy-start.1
  365.1 9.8 %collective-permute-start.13 = (f32[80,512]{1,0:T(8,128)}, f32[80,512]{1,0:T(8,128)}, u32[]{:S(2)}, u32[]{:S(2)}) collective-permute-start(f32[80,512]{1,0:T(8,128)} %get-tuple-element.72), channel_id=1, source_target_pairs={{0,2},{2,4},{4,6},{6,8},{8,10},{10,12},{12,14},{14,16},{16,18},{18... | collective-permute-start | bytes 491528 | tf_op jit(solution)/shard_map/ppermute | solution.py:214
  366.2 10.2 %collective-permute-start.16 = (f32[80,512]{1,0:T(8,128)}, f32[80,512]{1,0:T(8,128)}, u32[]{:S(2)}, u32[]{:S(2)}) collective-permute-start(f32[80,512]{1,0:T(8,128)} %get-tuple-element.71), channel_id=1, source_target_pairs={{0,30},{2,0},{4,2},{6,4},{8,6},{10,8},{12,10},{14,12},{16,14},{18,... | collective-permute-start | bytes 491528 | tf_op jit(solution)/shard_map/ppermute | solution.py:214
  382.4 6.1 %collective-permute-start.17 = (f32[48,512]{1,0:T(8,128)S(1)}, f32[48,512]{1,0:T(8,128)S(1)}, u32[]{:S(2)}, u32[]{:S(2)}) collective-permute-start(f32[48,512]{1,0:T(8,128)S(1)} %get-tuple-element.74), channel_id=1, source_target_pairs={{0,2},{1,3},{2,4},{3,5},{4,6},{5,7},{6,8},{7,9},{8,10},{9,11},{10,... | collective-permute-start | bytes 294920 | tf_op jit(solution)/shard_map/ppermute | solution.py:239
  383.5 5.1 %collective-permute-start.18 = (f32[48,512]{1,0:T(8,128)S(1)}, f32[48,512]{1,0:T(8,128)S(1)}, u32[]{:S(2)}, u32[]{:S(2)}) collective-permute-start(f32[48,512]{1,0:T(8,128)S(1)} %get-tuple-element.73), channel_id=1, source_target_pairs={{0,3},{1,2},{2,5},{3,4},{4,7},{5,6},{6,9},{7,8},{8,11},{9,10},{10,... | collective-permute-start | bytes 294920 | tf_op jit(solution)/shard_map/ppermute | solution.py:239
  384.5 5.0 %collective-permute-start.19 = (f32[48,512]{1,0:T(8,128)S(1)}, f32[48,512]{1,0:T(8,128)S(1)}, u32[]{:S(2)}, u32[]{:S(2)}) collective-permute-start(f32[48,512]{1,0:T(8,128)S(1)} %get-tuple-element.76), channel_id=1, source_target_pairs={{0,30},{1,31},{2,0},{3,1},{4,2},{5,3},{6,4},{7,5},{8,6},{9,7},{10,... | collective-permute-start | bytes 294920 | tf_op jit(solution)/shard_map/ppermute | solution.py:239
  385.2 6.4 %collective-permute-start.20 = (f32[48,512]{1,0:T(8,128)S(1)}, f32[48,512]{1,0:T(8,128)S(1)}, u32[]{:S(2)}, u32[]{:S(2)}) collective-permute-start(f32[48,512]{1,0:T(8,128)S(1)} %get-tuple-element.75), channel_id=1, source_target_pairs={{0,31},{1,30},{2,1},{3,0},{4,3},{5,2},{6,5},{7,4},{8,7},{9,6},{10,... | collective-permute-start | bytes 294920 | tf_op jit(solution)/shard_map/ppermute | solution.py:239

commit v5 on v4

--- a/solution.py
+++ b/solution.py
@@ -285,11 +285,12 @@
     came_c.append(send(cut))
     part = visit(*came_c[0], store, 0, unit, [word])
     both, came_c[1], part = together((both, came_c[1], part))
+    both = both.astype(jnp.bfloat16)
     returned = shifted(both[0], "ex", 1), shifted(both[1], "ex", -1)
     part = visit(*came_c[1], store, PIECES[0], unit, [word], part)
     part = visit(*came_c[2], store, PIECES[0] + PIECES[1], unit, returned, part)
-    upper_scores = [returned[0], to_owner(part[0], 1)]
-    lower_scores = [returned[1], to_owner(part[1], -1)]
+    upper_scores = [returned[0].astype(jnp.float32), to_owner(part[0], 1)]
+    lower_scores = [returned[1].astype(jnp.float32), to_owner(part[1], -1)]
 
     scores = jnp.stack(
         [jnp.concatenate(upper_scores), own_scores, jnp.concatenate(lower_scores)]

time: 395 us -> 392 us (level)
  transfers between devices with their start and end apart: 21 -> 21, of which waited for: 10 -> 9; matrix products, arithmetic and copies ran while one was open for 4% -> 4% of each run, Pallas kernels for 29% -> 29%
where the time goes in v5:
time: 392 us; the launch traced here: 391 us
  waiting for transfers between devices  229 us (58%)
  Pallas kernels  118 us (30%)
  starting transfers between devices  23.7 us (6%)
  local copies, waits for them, and re-layouts  14.6 us (4%)
  other arithmetic  5.55 us (1%)
    ppermute x14, waiting for transfers between devices, shifted(): return lax.ppermute(value, axis, pairs)  224 us
    pallas_call x4, Pallas kernels, visit(): pl.pallas_call(functools.partial(visit_kernel, len(words)), grid=(width /...  45.4 us
    pallas_call x1, Pallas kernels, own(): pl.pallas_call(functools.partial(own_kernel, bounds), grid=(modules,), in...  37.8 us
    pallas_call x1, Pallas kernels, visit_raw(): pl.pallas_call(functools.partial(visit_raw_kernel, len(pieces)), grid=(mo...  35.3 us
    ppermute x14, starting transfers between devices, shifted(): return lax.ppermute(value, axis, pairs)  14.6 us
    slice x3, local copies, waits for them, and re-layouts, body(): cuts.append(c[..., start * unit:(start + count) * unit])  9.06 us
  transfers between devices with their start and end apart: 21, of which 9 were waited for; matrix products, arithmetic and copies ran while one was open for 4% of the time, Pallas kernels for 29%

profile of v5, /device:TPU:1, one launch (start us, length us, event | category | flops | bytes accessed | tf_op | source)
XLA Modules:
  0.0 391.4 jit_solution(10907939601198787443)
XLA Ops:
  0.0 1.7 slice.44
  1.7 0.1 collective-permute-start
  1.8 2.6 collective-permute-start.1
  4.5 37.8 %own.1 = (bf16[2,64,32768]{2,1,0:T(8,128)(2,1)}, bf16[2,48,32768]{2,1,0:T(8,128)(2,1)}, f32[2,128,512]{2,1,0:T(8,128)}) custom-call(bf16[256,32768]{1,0:T(8,128)(2,1)} %x_ref, bf16[8,64,64]{2,1,0:T(8,128)(2,1)} %refs_2_.1, bf16[8,64,64]{2,1,0:T(8,128)(2,1)} %refs_3_.1, bf16[512,32768]{1,0:T(8,128)(2,1)} %slab_ref.9), custom_call_target="tpu_custom_call" | custom-call | tf_op jit(solution)/shard_map/own/pallas_call | solution.py:108
  42.2 4.3 %slice.35 = bf16[2,48,20480]{2,1,0:T(8,128)(2,1)} slice(bf16[2,48,32768]{2,1,0:T(8,128)(2,1)} %get-tuple-element.41), slice={[0:2], [0:48], [0:20480]} | slice | bytes 7864320 | tf_op jit(solution)/shard_map/slice | solution.py:264
  46.5 2.7 slice.36
  49.2 2.1 slice.37
  51.3 2.9 collective-permute-start.2
  54.2 0.8 collective-permute-done.2.refs_5_
  55.0 0.3 collective-permute-start.5
  55.4 1.4 collective-permute-start.6
  56.8 3.0 collective-permute-start.3
  59.8 1.3 collective-permute-start.7
  61.1 35.3 %visit_raw.1 = f32[2,2,16,512]{3,2,1,0:T(8,128)} custom-call(bf16[2,16,32768]{2,1,0:T(8,128)(2,1)} %copy-done, bf16[2,16,32768]{2,1,0:T(8,128)(2,1)} %collective-permute-done.1.refs_1_, bf16[8,64,64]{2,1,0:T(8,128)(2,1)} %refs_2_.1, bf16[8,64,64]{2,1,0:T(8,128)(2,1)} %refs_3_.1, bf16[512,32768]{1,0:T(8,128)(2,1)} %slab_ref.9, bf16[16,128]{1,0:T(8,128)(2,1)} %copy-done.9), custom_call_target="tpu_custom_call" | custom-call | tf_op jit(solution)/shard_map/visit_raw/pallas_call | solution.py:156
  96.5 183.8 %collective-permute-done.5.upper_ref = bf16[2,64,32768]{2,1,0:T(8,128)(2,1)} collective-permute-done((bf16[2,64,32768]{2,1,0:T(8,128)(2,1)}, bf16[2,64,32768]{2,1,0:T(8,128)(2,1)}, u32[]{:S(2)}, u32[]{:S(2)}) %collective-permute-start.5) | collective-permute-done | bytes 8388640 | tf_op jit(solution)/shard_map/ppermute | solution.py:214
  280.2 0.7 slice_bitcast_fusion.2
  281.0 1.2 collective-permute-done.8.rest_0_
  282.2 0.2 collective-permute-start.10
  282.4 1.6 collective-permute-start.11
  284.0 19.9 %visit.4 = f32[2,2,64,512]{3,2,1,0:T(8,128)} custom-call(bf16[2,64,32768]{2,1,0:T(8,128)(2,1)} %collective-permute-done.5.upper_ref, bf16[2,64,32768]{2,1,0:T(8,128)(2,1)} %collective-permute-done.6.lower_ref, bf16[512,32768]{1,0:T(8,128)(2,1)} %slab_ref.9, bf16[64,128]{1,0:T(8,128)(2,1)} %copy-done.8), custom_call_target="tpu_custom_call" | custom-call | tf_op jit(solution)/shard_map/visit/pallas_call | solution.py:194
  303.9 1.0 fusion.1
  304.9 1.3 collective-permute-start.9
  306.1 33.1 %collective-permute-done.3.upper_ref = bf16[2,48,20480]{2,1,0:T(8,128)(2,1)} collective-permute-done((bf16[2,48,20480]{2,1,0:T(8,128)(2,1)}, bf16[2,48,20480]{2,1,0:T(8,128)(2,1)}, u32[]{:S(2)}, u32[]{:S(2)}) %collective-permute-start.3) | collective-permute-done | bytes 3932192 | tf_op jit(solution)/shard_map/ppermute | solution.py:214
  339.2 0.7 slice_bitcast_fusion.3
  339.9 1.6 fusion.4
  341.6 1.2 collective-permute-done.12.rest_0_
  342.8 0.2 collective-permute-start.14
  342.9 1.6 collective-permute-start.15
  344.6 0.1 broadcast_in_dim.6
  344.7 0.1 reshape.21
  344.8 13.6 %visit.5.rest_1_ = f32[2,2,48,512]{3,2,1,0:T(8,128)} custom-call(bf16[2,48,20480]{2,1,0:T(8,128)(2,1)} %collective-permute-done.3.upper_ref, bf16[2,48,20480]{2,1,0:T(8,128)(2,1)} %collective-permute-done.4.lower_ref, bf16[512,32768]{1,0:T(8,128)(2,1)} %slab_ref.9, bf16[48,128]{1,0:T(8,128)(2,1)} %copy-done.7), custom_call_target="tpu_custom_call" | custom-call | tf_op jit(solution)/shard_map/visit/pallas_call | solution.py:194
  358.4 6.0 %collective-permute-done.10.upper_ref = bf16[2,48,8192]{2,1,0:T(8,128)(2,1)S(1)} collective-permute-done((bf16[2,48,8192]{2,1,0:T(8,128)(2,1)}, bf16[2,48,8192]{2,1,0:T(8,128)(2,1)S(1)}, u32[]{:S(2)}, u32[]{:S(2)}) %collective-permute-start.10) | collective-permute-done | bytes 1572896 | tf_op jit(solution)/shard_map/ppermute | solution.py:214
  364.4 0.7 slice_bitcast_fusion
  365.1 1.0 collective-permute-start.13
  366.2 0.3 copy.7
  366.5 6.9 %visit.6.rest_2_ = f32[2,2,48,512]{3,2,1,0:T(8,128)} custom-call(bf16[2,48,8192]{2,1,0:T(8,128)(2,1)} %copy-done.1, bf16[2,48,8192]{2,1,0:T(8,128)(2,1)} %copy-done.2, bf16[512,32768]{1,0:T(8,128)(2,1)} %slab_ref.9, bf16[48,128]{1,0:T(8,128)(2,1)} %copy-done.7, f32[2,2,48,512]{3,2,1,0:T(8,128)} %visit.5.rest_1_), custom_call_target="tpu_custom_call" | custom-call | tf_op jit(solution)/shard_map/visit/pallas_call | solution.py:194
  373.4 0.4 collective-permute-done.14.upper_ref
  373.8 0.9 collective-permute-done.16.rest_1_
  374.7 5.0 %visit.7 = f32[2,2,48,512]{3,2,1,0:T(8,128)} custom-call(bf16[2,48,4096]{2,1,0:T(8,128)(2,1)} %collective-permute-done.14.upper_ref, bf16[2,48,4096]{2,1,0:T(8,128)(2,1)} %collective-permute-done.15.lower_ref, bf16[512,32768]{1,0:T(8,128)(2,1)} %slab_ref.9, bf16[80,512]{1,0:T(8,128)(2,1)} %copy-done.6, bf16[80,512]{1,0:T(8,128)(2,1)} %collective-permute-done.16.rest_1_, ...), custom_call_target="tpu_custom_call" | custom-call | tf_op jit(solution)/shard_map/visit/pallas_call | solution.py:194
  379.7 1.0 fusion.5
  380.7 1.6 collective-permute-start.17
  382.3 1.0 collective-permute-start.18
  383.4 0.7 collective-permute-start.19
  384.0 2.9 collective-permute-start.20
  386.9 0.9 convert_element_type.13
  387.8 0.9 convert_element_type.14
  388.8 1.6 collective-permute-done.20
  390.4 1.0 maximum_multiply_fusion
  (51 shorter events, 0.4 us)
Async XLA Ops:
  1.7 49.6 %collective-permute-start = (bf16[2,16,32768]{2,1,0:T(8,128)(2,1)S(1)}, bf16[2,16,32768]{2,1,0:T(8,128)(2,1)S(1)}, u32[]{:S(2)}, u32[]{:S(2)}) collective-permute-start(bf16[2,16,32768]{2,1,0:T(8,128)(2,1)S(1)} %slice.44), channel_id=1, source_target_pairs={{0,30},{2,0},{4,2},{6,4},{8,6},{10,8},{12,10},{14,12},{16,14},{18,... | collective-permute-start | bytes 6291464 | tf_op jit(solution)/shard_map/ppermute | solution.py:214
  1.8 49.5 %collective-permute-start.1 = (bf16[2,16,32768]{2,1,0:T(8,128)(2,1)S(1)}, bf16[2,16,32768]{2,1,0:T(8,128)(2,1)}, u32[]{:S(2)}, u32[]{:S(2)}) collective-permute-start(bf16[2,16,32768]{2,1,0:T(8,128)(2,1)S(1)} %slice.44), channel_id=1, source_target_pairs={{0,2},{2,4},{4,6},{6,8},{8,10},{10,12},{12,14},{14,16},{16,18},{18... | collective-permute-start | bytes 6291464 | tf_op jit(solution)/shard_map/ppermute | solution.py:214
  46.5 13.3 %copy-start.5 = (f32[2,128,512]{2,1,0:T(8,128)S(1)}, f32[2,128,512]{2,1,0:T(8,128)}, u32[]{:S(2)}) copy-start(f32[2,128,512]{2,1,0:T(8,128)} %get-tuple-element.49) | copy-start | bytes 1572868
  51.3 9.8 %copy-start = (bf16[2,16,32768]{2,1,0:T(8,128)(2,1)}, bf16[2,16,32768]{2,1,0:T(8,128)(2,1)S(1)}, u32[]{:S(2)}) copy-start(bf16[2,16,32768]{2,1,0:T(8,128)(2,1)S(1)} %collective-permute-done.refs_0_) | copy-start | bytes 6291460
  51.3 3.7 collective-permute-start.2
  55.0 6.1 %copy-start.9 = (bf16[16,128]{1,0:T(8,128)(2,1)}, bf16[16,128]{1,0:T(8,128)(2,1)S(1)}, u32[]{:S(2)}) copy-start(bf16[16,128]{1,0:T(8,128)(2,1)S(1)} %collective-permute-done.2.refs_5_) | copy-start | bytes 12292
  55.0 225.2 %collective-permute-start.5 = (bf16[2,64,32768]{2,1,0:T(8,128)(2,1)}, bf16[2,64,32768]{2,1,0:T(8,128)(2,1)}, u32[]{:S(2)}, u32[]{:S(2)}) collective-permute-start(bf16[2,64,32768]{2,1,0:T(8,128)(2,1)} %get-tuple-element.45), channel_id=1, source_target_pairs={{0,30},{2,0},{4,2},{6,4},{8,6},{10,8},{12,10},{14,12},{16,14},{18,... | collective-permute-start | bytes 25165832 | tf_op jit(solution)/shard_map/ppermute | solution.py:214
  55.4 225.6 %collective-permute-start.6 = (bf16[2,64,32768]{2,1,0:T(8,128)(2,1)}, bf16[2,64,32768]{2,1,0:T(8,128)(2,1)}, u32[]{:S(2)}, u32[]{:S(2)}) collective-permute-start(bf16[2,64,32768]{2,1,0:T(8,128)(2,1)} %get-tuple-element.45), channel_id=1, source_target_pairs={{0,2},{2,4},{4,6},{6,8},{8,10},{10,12},{12,14},{14,16},{16,18},{18... | collective-permute-start | bytes 25165832 | tf_op jit(solution)/shard_map/ppermute | solution.py:214
  56.8 282.4 %collective-permute-start.3 = (bf16[2,48,20480]{2,1,0:T(8,128)(2,1)}, bf16[2,48,20480]{2,1,0:T(8,128)(2,1)}, u32[]{:S(2)}, u32[]{:S(2)}) collective-permute-start(bf16[2,48,20480]{2,1,0:T(8,128)(2,1)} %slice.35), channel_id=1, source_target_pairs={{0,30},{2,0},{4,2},{6,4},{8,6},{10,8},{12,10},{14,12},{16,14},{18,... | collective-permute-start | bytes 11796488 | tf_op jit(solution)/shard_map/ppermute | solution.py:214
  59.8 281.8 %collective-permute-start.4 = (bf16[2,48,20480]{2,1,0:T(8,128)(2,1)}, bf16[2,48,20480]{2,1,0:T(8,128)(2,1)}, u32[]{:S(2)}, u32[]{:S(2)}) collective-permute-start(bf16[2,48,20480]{2,1,0:T(8,128)(2,1)} %slice.35), channel_id=1, source_target_pairs={{0,2},{2,4},{4,6},{6,8},{8,10},{10,12},{12,14},{14,16},{16,18},{18... | collective-permute-start | bytes 11796488 | tf_op jit(solution)/shard_map/ppermute | solution.py:214
  59.8 36.6 %collective-permute-start.7 = (f32[128,512]{1,0:T(8,128)S(1)}, f32[128,512]{1,0:T(8,128)S(1)}, u32[]{:S(2)}, u32[]{:S(2)}) collective-permute-start(f32[128,512]{1,0:T(8,128)S(1)} %dynamic-slice_bitcast_fusion), channel_id=1, source_target_pairs={{0,1},{1,0},{2,3},{3,2},{4,5},{5,4},{6,7},{7,6},{8,9},{9,8},{10,11... | collective-permute-start | bytes 786440 | tf_op jit(solution)/shard_map/ppermute | solution.py:214
  280.9 22.9 %copy-start.3 = (f32[2,2,16,512]{3,2,1,0:T(8,128)S(1)}, f32[2,2,16,512]{3,2,1,0:T(8,128)}, u32[]{:S(2)}) copy-start(f32[2,2,16,512]{3,2,1,0:T(8,128)} %visit_raw.1) | copy-start | bytes 393220
  281.0 63.6 %copy-start.10 = (s32[8,24]{1,0:T(8,128)S(1)}, s32[8,24]{1,0:T(8,128)}, u32[]{:S(2)}) copy-start(s32[8,24]{1,0:T(8,128)} %param.9) | copy-start | bytes 2308
  281.0 1.2 collective-permute-start.8
  282.2 1.8 copy-start.8
  282.2 82.2 %collective-permute-start.10 = (bf16[2,48,8192]{2,1,0:T(8,128)(2,1)}, bf16[2,48,8192]{2,1,0:T(8,128)(2,1)S(1)}, u32[]{:S(2)}, u32[]{:S(2)}) collective-permute-start(bf16[2,48,8192]{2,1,0:T(8,128)(2,1)} %slice.36), channel_id=1, source_target_pairs={{0,30},{2,0},{4,2},{6,4},{8,6},{10,8},{12,10},{14,12},{16,14},{18,... | collective-permute-start | bytes 4718600 | tf_op jit(solution)/shard_map/ppermute | solution.py:214
  282.4 82.0 %collective-permute-start.11 = (bf16[2,48,8192]{2,1,0:T(8,128)(2,1)}, bf16[2,48,8192]{2,1,0:T(8,128)(2,1)S(1)}, u32[]{:S(2)}, u32[]{:S(2)}) collective-permute-start(bf16[2,48,8192]{2,1,0:T(8,128)(2,1)} %slice.36), channel_id=1, source_target_pairs={{0,2},{2,4},{4,6},{6,8},{8,10},{10,12},{12,14},{14,16},{16,18},{18... | collective-permute-start | bytes 4718600 | tf_op jit(solution)/shard_map/ppermute | solution.py:214
  304.9 35.1 %collective-permute-start.9 = (f32[2,80,512]{2,1,0:T(8,128)S(1)}, f32[2,80,512]{2,1,0:T(8,128)S(1)}, u32[]{:S(2)}, u32[]{:S(2)}) collective-permute-start(f32[2,80,512]{2,1,0:T(8,128)S(1)} %fusion.1), channel_id=1, source_target_pairs={{0,1},{1,0},{2,3},{3,2},{4,5},{5,4},{6,7},{7,6},{8,9},{9,8},{10,11... | collective-permute-start | bytes 983048 | tf_op jit(solution)/shard_map/ppermute | solution.py:214
  341.6 1.2 collective-permute-start.12
  342.8 2.0 copy-start.7
  342.8 31.0 %collective-permute-start.14 = (bf16[2,48,4096]{2,1,0:T(8,128)(2,1)}, bf16[2,48,4096]{2,1,0:T(8,128)(2,1)}, u32[]{:S(2)}, u32[]{:S(2)}) collective-permute-start(bf16[2,48,4096]{2,1,0:T(8,128)(2,1)} %slice.37), channel_id=1, source_target_pairs={{0,30},{2,0},{4,2},{6,4},{8,6},{10,8},{12,10},{14,12},{16,14},{18,... | collective-permute-start | bytes 2359304 | tf_op jit(solution)/shard_map/ppermute | solution.py:214
  342.9 30.9 %collective-permute-start.15 = (bf16[2,48,4096]{2,1,0:T(8,128)(2,1)}, bf16[2,48,4096]{2,1,0:T(8,128)(2,1)}, u32[]{:S(2)}, u32[]{:S(2)}) collective-permute-start(bf16[2,48,4096]{2,1,0:T(8,128)(2,1)} %slice.37), channel_id=1, source_target_pairs={{0,2},{2,4},{4,6},{6,8},{8,10},{10,12},{12,14},{14,16},{16,18},{18... | collective-permute-start | bytes 2359304 | tf_op jit(solution)/shard_map/ppermute | solution.py:214
  344.8 19.6 %copy-start.4 = (bf16[2,80,512]{2,1,0:T(8,128)(2,1)S(1)}, bf16[2,80,512]{2,1,0:T(8,128)(2,1)}, u32[]{:S(2)}) copy-start(bf16[2,80,512]{2,1,0:T(8,128)(2,1)} %fusion.4) | copy-start | bytes 491524
  364.4 2.1 copy-start.1
  364.4 1.7 copy-start.2
  365.1 8.7 %collective-permute-start.13 = (bf16[80,512]{1,0:T(8,128)(2,1)}, bf16[80,512]{1,0:T(8,128)(2,1)S(1)}, u32[]{:S(2)}, u32[]{:S(2)}) collective-permute-start(bf16[80,512]{1,0:T(8,128)(2,1)} %get-tuple-element.76), channel_id=1, source_target_pairs={{0,2},{2,4},{4,6},{6,8},{8,10},{10,12},{12,14},{14,16},{16,18},{18... | collective-permute-start | bytes 245768 | tf_op jit(solution)/shard_map/ppermute | solution.py:214
  366.1 8.6 %collective-permute-start.16 = (bf16[80,512]{1,0:T(8,128)(2,1)}, bf16[80,512]{1,0:T(8,128)(2,1)}, u32[]{:S(2)}, u32[]{:S(2)}) collective-permute-start(bf16[80,512]{1,0:T(8,128)(2,1)} %get-tuple-element.75), channel_id=1, source_target_pairs={{0,30},{2,0},{4,2},{6,4},{8,6},{10,8},{12,10},{14,12},{16,14},{18,... | collective-permute-start | bytes 245768 | tf_op jit(solution)/shard_map/ppermute | solution.py:214
  373.8 0.9 copy-start.6
  380.7 8.0 %collective-permute-start.17 = (f32[48,512]{1,0:T(8,128)S(1)}, f32[48,512]{1,0:T(8,128)S(1)}, u32[]{:S(2)}, u32[]{:S(2)}) collective-permute-start(f32[48,512]{1,0:T(8,128)S(1)} %get-tuple-element.72), channel_id=1, source_target_pairs={{0,2},{1,3},{2,4},{3,5},{4,6},{5,7},{6,8},{7,9},{8,10},{9,11},{10,... | collective-permute-start | bytes 294920 | tf_op jit(solution)/shard_map/ppermute | solution.py:239
  382.3 6.4 %collective-permute-start.18 = (f32[48,512]{1,0:T(8,128)S(1)}, f32[48,512]{1,0:T(8,128)S(1)}, u32[]{:S(2)}, u32[]{:S(2)}) collective-permute-start(f32[48,512]{1,0:T(8,128)S(1)} %get-tuple-element.71), channel_id=1, source_target_pairs={{0,3},{1,2},{2,5},{3,4},{4,7},{5,6},{6,9},{7,8},{8,11},{9,10},{10,... | collective-permute-start | bytes 294920 | tf_op jit(solution)/shard_map/ppermute | solution.py:239
  383.4 5.4 %collective-permute-start.19 = (f32[48,512]{1,0:T(8,128)S(1)}, f32[48,512]{1,0:T(8,128)S(1)}, u32[]{:S(2)}, u32[]{:S(2)}) collective-permute-start(f32[48,512]{1,0:T(8,128)S(1)} %get-tuple-element.74), channel_id=1, source_target_pairs={{0,30},{1,31},{2,0},{3,1},{4,2},{5,3},{6,4},{7,5},{8,6},{9,7},{10,... | collective-permute-start | bytes 294920 | tf_op jit(solution)/shard_map/ppermute | solution.py:239
  384.0 6.3 %collective-permute-start.20 = (f32[48,512]{1,0:T(8,128)S(1)}, f32[48,512]{1,0:T(8,128)S(1)}, u32[]{:S(2)}, u32[]{:S(2)}) collective-permute-start(f32[48,512]{1,0:T(8,128)S(1)} %get-tuple-element.73), channel_id=1, source_target_pairs={{0,31},{1,30},{2,1},{3,0},{4,3},{5,2},{6,5},{7,4},{8,7},{9,6},{10,... | collective-permute-start | bytes 294920 | tf_op jit(solution)/shard_map/ppermute | solution.py:239
